TPU v7x, 32 devices: a whole 2x2x4 slice. The times are simulated.
32 devices in a mesh: groups: 2 (over y), chan: 4 (over z), win: 4 (over x, core).
Axes of the slice: x: 2, y: 2, z: 4, core: 2. Of those that a mesh axis runs over, the one named last changes fastest.
Arguments:
- tokens: bfloat16 [8, 1024, 512], P(('groups', 'win'), 'chan'), parts along dimension 0, may hold values from -6 to 6
- head_weight: bfloat16 [512, 1024], replicated, may hold values from -0.25 to 0.25
- target: bfloat16 [8, 512, 2048], P(('groups', 'win'), 'chan'), parts along dimension 0, may hold values from -6 to 6
- target_amp: bfloat16 [8, 512, 2048], P(('groups', 'win'), 'chan'), parts along dimension 0, may hold values from 0.29882812 to 3
- patch_ranks: int32 [8, 1024], P(('groups', 'win'), 'chan'), parts along dimension 0, may hold values from 0 to 1023, each once within a row
Outputs:
- grad_tokens: bfloat16 [8, 1024, 512], P(('groups', 'win'), 'chan'), parts along dimension 0
- grad_weight: float32 [1024, 1024], P(('groups', 'chan'), 'win'), parts along dimension 0
There are 2 independent parts, one for each index of `groups`. A program takes and returns all parts, laid end to end along the dimension named above; an argument that names none is the same for every part. Nothing has to cross between parts.
Inputs may be any that keep to these rules, and one draw needn't show every extreme that they name: `patch_ranks`: each window's row is a permutation of 0 to 1023; a patch is masked exactly when its rank is 256 or more.
All inputs are finite; a program needn't handle non-finite values.
Results may differ from a plain program's by a relative error of at most 0.0052.
Values sent between devices are 32-bit elements; how exact they have to be, the bound alone decides.
A program may use at most 128 MiB of HBM per device.

v0:
```python
from functools import partial
import math

import jax
import jax.numpy as jnp
import numpy as np
from jax import lax
from jax.sharding import PartitionSpec as P

PATCH_C = 16
PATCH_S = 64
DENSE_LIMIT = 1024
F32 = jnp.float32
BF16 = jnp.bfloat16

product = partial(jnp.einsum, precision=lax.Precision.HIGHEST)


def two_parts(table):
    high = table.astype(BF16)
    low = (table - high.astype(np.float64)).astype(BF16)
    return high, low


def time_table(samples, blocks):
    half = samples // 2
    freq = np.arange(half)[:, None] * np.arange(samples)[None, :] % samples
    angles = 2.0 * np.pi / samples * freq
    cosine = np.cos(angles)
    sine = -np.sin(angles)
    sine[0] = 1.0 - 2.0 * (np.arange(samples) % 2)
    both = np.stack([cosine.reshape(blocks, -1, samples), sine.reshape(blocks, -1, samples)], axis=1)
    return both.reshape(samples, samples)


def chan_table(channels, blocks):
    angles = 2.0 * np.pi / channels * (np.arange(channels)[:, None] * np.arange(channels)[None, :] % channels)
    cosine = np.cos(angles)
    sine = np.sin(angles)
    table = np.stack([np.stack([cosine, sine], axis=1), np.stack([-sine, cosine], axis=1)], axis=0)
    table = table.reshape(2 * channels, 2, blocks, channels // blocks).transpose(0, 2, 1, 3)
    return table.reshape(2 * channels, 2 * channels)


def negation(length):
    table = np.zeros((length, length), np.float32)
    table[np.arange(length), -np.arange(length) % length] = 1.0
    return table.astype(BF16)


def dot(left, right, dims=((1,), (0,))):
    return lax.dot_general(left, right, (dims, ((), ())), preferred_element_type=F32)


def split(values):
    high = values.astype(BF16)
    return high, (values - high.astype(F32)).astype(BF16)


def factor_pair(length):
    first = int(math.isqrt(length))
    while length % first:
        first -= 1
    return (first, length // first)


def section_one(length, direction):
    index = jnp.arange(length, dtype=jnp.int32)
    angles = direction * 2.0 * math.pi / length * (index[:, None] * index[None, :] % length).astype(F32)
    cosine = jnp.cos(angles)
    sine = jnp.sin(angles)
    upper = jnp.stack([cosine, sine], axis=1)
    lower = jnp.stack([-sine, cosine], axis=1)
    return jnp.stack([upper, lower], axis=0)


def section_two(first, second, direction):
    length = first * second
    outer = jnp.arange(first, dtype=jnp.int32)[:, None, None]
    inner = jnp.arange(second, dtype=jnp.int32)[None, :, None]
    final = jnp.arange(second, dtype=jnp.int32)[None, None, :]
    phase = (outer * inner + first * inner * final) % length
    angles = direction * 2.0 * math.pi / length * phase.astype(F32)
    cosine = jnp.cos(angles)
    sine = jnp.sin(angles)
    upper = jnp.stack([cosine, sine], axis=2)
    lower = jnp.stack([-sine, cosine], axis=2)
    return jnp.stack([upper, lower], axis=0)


def factored_transform(spectrum, direction):
    _, length, columns = spectrum.shape
    first, second = factor_pair(length)
    shaped = spectrum.reshape(2, first, second, columns)
    section = product("rabm,rask->skbm", shaped, section_one(length=first, direction=direction))
    result = product("skbm,skbtj->tjkm", section, section_two(first, second, direction))
    return result.reshape(2, length, columns)


def chan_forward(rows, channels, blocks):
    if channels <= DENSE_LIMIT:
        table = chan_table(channels, blocks)
        high, low = two_parts(table)
        rows_high, rows_low = split(rows)
        return dot(high, rows_high) + dot(high, rows_low) + dot(low, rows_high)
    columns = rows.shape[1]
    shaped = rows.reshape(blocks, 2, channels // blocks, columns).transpose(1, 0, 2, 3)
    return factored_transform(shaped.reshape(2, channels, columns), -1.0).reshape(2 * channels, columns)


def chan_inverse(rows, channels, blocks):
    if channels <= DENSE_LIMIT:
        high, _ = two_parts(chan_table(channels, blocks))
        return dot(high, rows.astype(BF16), ((0,), (0,)))
    columns = rows.shape[1]
    shaped = factored_transform(rows.reshape(2, channels, columns), 1.0)
    shaped = shaped.reshape(2, blocks, channels // blocks, columns).transpose(1, 0, 2, 3)
    return shaped.reshape(2 * channels, columns)


def per_device(tokens, head_weight, target, target_amp, patch_ranks):
    blocks = lax.axis_size("chan")
    all_windows = lax.axis_size("win")
    tokens, target, target_amp, patch_ranks = tokens[0], target[0], target_amp[0], patch_ranks[0]
    local_patches, width = tokens.shape
    rows, samples = target.shape
    channels = rows * blocks
    half = samples // 2
    cols = half // blocks
    chan_patches = rows // PATCH_C
    sample_patches = samples // PATCH_S
    keep_count = local_patches * blocks // 4
    norm = 1.0 / math.sqrt(channels * samples)
    here = lax.axis_index("chan")

    upper = dot(target_amp[:, half:], negation(half))
    amp = jnp.stack([target_amp[:, :half].astype(F32), upper])
    amp = amp.reshape(2, rows, blocks, cols).transpose(2, 0, 1, 3)
    amp = lax.all_to_all(amp, "chan", split_axis=0, concat_axis=0, tiled=True)

    patches = dot(tokens, head_weight).astype(BF16)
    image = patches.reshape(chan_patches, sample_patches, PATCH_C, PATCH_S)
    image = image.transpose(0, 2, 1, 3).reshape(rows, samples)
    masked = (patch_ranks >= keep_count).reshape(chan_patches, 1, sample_patches, 1)
    pixel_mask = jnp.broadcast_to(masked, (chan_patches, PATCH_C, sample_patches, PATCH_S)).reshape(rows, samples)
    composite = jnp.where(pixel_mask, image, target)

    high, low = two_parts(time_table(samples, blocks))
    spectrum = dot(composite, high, ((1,), (1,))) + dot(composite, low, ((1,), (1,)))
    spectrum = spectrum.reshape(rows, blocks, 2, cols).transpose(1, 2, 0, 3)
    spectrum = lax.all_to_all(spectrum, "chan", split_axis=0, concat_axis=0, tiled=True)

    lane = lax.broadcasted_iota(jnp.int32, (1, 128), 1)
    first_col = spectrum[:, :, :, :1]
    extra = jnp.where(lane == 0, first_col[:, 0], 0.0) + jnp.where(lane == 1, first_col[:, 1], 0.0)
    extra = jnp.stack([extra, jnp.zeros_like(extra)], axis=1)
    stacked = jnp.concatenate([spectrum, extra], axis=3).reshape(2 * channels, cols + 128)
    amp_low = amp[:, 0].reshape(channels, cols)
    amp_up = amp[:, 1].reshape(channels, cols)
    amp_sum = amp_low + dot(negation(channels).astype(F32), amp_up)
    amp_extra = jnp.where(lane == 0, amp_low[:, :1], amp_up[:, :1])
    amp_all = jnp.concatenate([amp_sum, amp_extra], axis=1)

    freq = chan_forward(stacked, channels, blocks).reshape(2, channels, cols + 128) * norm
    inverse_amp = lax.rsqrt(freq[0] * freq[0] + freq[1] * freq[1] + 1.0)
    scaled = freq * (inverse_amp * amp_all * norm)
    back = chan_inverse(scaled.reshape(2 * channels, cols + 128), channels, blocks)
    back = back.reshape(blocks, 2, rows, cols + 128)
    edge = jnp.stack([back[:, 0, :, cols : cols + 1], back[:, 0, :, cols + 1 : cols + 2]], axis=1)
    column = lax.broadcasted_iota(jnp.int32, (1, 1, 1, cols), 3)
    returned = jnp.where((column == 0) & (here == 0), edge, back[:, :, :, :cols])
    returned = lax.all_to_all(returned, "chan", split_axis=0, concat_axis=0, tiled=True)

    returned = returned.transpose(2, 0, 1, 3).reshape(rows, samples)
    returned_high, returned_low = split(returned)
    pulled = dot(returned_high, high) + dot(returned_low, high)
    grad_image = jnp.where(pixel_mask, (composite.astype(F32) - pulled) * (1.0 / all_windows), 0.0)
    grad_patches = grad_image.astype(BF16).reshape(chan_patches, PATCH_C, sample_patches, PATCH_S)
    grad_patches = grad_patches.transpose(0, 2, 1, 3).reshape(local_patches, PATCH_C * PATCH_S)
    grad_tokens = dot(grad_patches, head_weight, ((1,), (1,))).astype(BF16)
    grad_weight = dot(tokens, grad_patches, ((0,), (0,)))
    grad_weight = lax.psum_scatter(grad_weight, "win", scatter_dimension=1, tiled=True)
    grad_weight = lax.psum_scatter(grad_weight, "chan", scatter_dimension=0, tiled=True)
    return (grad_tokens[None], grad_weight)


def solution(mesh):
    in_specs = (
        P(("groups", "win"), "chan", None),
        P(),
        P(("groups", "win"), "chan", None),
        P(("groups", "win"), "chan", None),
        P(("groups", "win"), "chan"),
    )
    out_specs = (P(("groups", "win"), "chan", None), P(("groups", "chan"), "win"))
    return jax.shard_map(
        per_device, mesh=mesh, in_specs=in_specs, out_specs=out_specs, check_vma=False
    )
```

profile of v0, /device:TPU:0, one launch (start us, length us, event | category | flops | bytes accessed | tf_op | source)
XLA Modules:
  0.0 192.0 jit_solution(358162768252641495)
XLA Ops:
  7.2 1.1 slice_convert_fusion
  8.3 2.3 %fusion.20 = f32[1024,128]{1,0:T(8,128)S(1)} fusion(bf16[1024,1024]{1,0:T(8,128)(2,1)} %constant.37.clone, bf16[128,2048]{1,0:T(8,128)(2,1)} %bitcast.122), kind=kOutput, calls=%fused_computation.47 | convolution fusion | flops 268435456 | bytes 2883584 | tf_op jit(solution)/shard_map/dot_general | solution.py:52
  10.8 1.1 maximum_bitcast_fusion
  11.9 6.5 %all-to-all-start.1 = ((f32[4,2,128,256]{2,3,1,0:T(8,128)}), f32[4,2,128,256]{2,3,1,0:T(8,128)S(1)}, u32[]{:S(2)}, u32[]{:S(2)}) async-start(f32[4,2,128,256]{2,3,1,0:T(8,128)} %maximum_bitcast_fusion), calls=%async_computation.1 | async-start | bytes 2097152 | tf_op jit(solution)/shard_map/all_to_all | solution.py:139
  18.7 1.3 reshape.149
  20.4 1.6 reshape.150
  22.0 2.5 %copy.37 = bf16[8,16,32,64]{3,2,1,0:T(8,128)(2,1)} copy(bf16[8,16,32,64]{3,1,2,0:T(8,128)(2,1)} %bitcast.114) | data formatting | bytes 1048576 | tf_op jit(solution)/shard_map/transpose | solution.py:143
  24.5 2.0 %reshape.151 = bf16[128,2048]{1,0:T(8,128)(2,1)S(1)} reshape(bf16[8,16,32,64]{3,2,1,0:T(8,128)(2,1)} %copy.37) | data formatting | bytes 1048576 | tf_op jit(solution)/shard_map/reshape | solution.py:143
  26.6 1.2 bitcast_select_fusion
  27.7 6.2 %fusion.24 = f32[128,2048]{1,0:T(8,128)S(1)} fusion(bf16[128,2048]{1,0:T(8,128)(2,1)S(1)} %bitcast_select_fusion, bf16[2048,2048]{1,0:T(8,128)(2,1)} %constant.38.clone), kind=kOutput, calls=%fused_computation.57 | convolution fusion | flops 1073741824 | bytes 9961472 | tf_op jit(solution)/shard_map/dot_general | solution.py:52
  34.0 7.3 %convolution_add_fusion.1 = f32[128,2048]{1,0:T(8,128)} fusion(f32[128,2048]{1,0:T(8,128)S(1)} %fusion.24, bf16[128,2048]{1,0:T(8,128)(2,1)S(1)} %bitcast_select_fusion, bf16[2048,2048]{1,0:T(8,128)(2,1)} %constant.39.clone), kind=kOutput, calls=%fused_computation.1 | convolution fusion | flops 1074003968 | bytes 11010048 | tf_op jit(solution)/shard_map/dot_general | solution.py:52
  41.3 3.1 %reshape.152 = f32[128,4,2,256]{3,2,1,0:T(2,128)} reshape(f32[128,2048]{1,0:T(8,128)} %convolution_add_fusion.1) | data formatting | bytes 2097152 | tf_op jit(solution)/shard_map/reshape | solution.py:150
  44.4 2.5 %copy.60 = f32[128,4,2,256]{3,0,2,1:T(8,128)} copy(f32[128,4,2,256]{3,2,1,0:T(2,128)} %reshape.152) | data formatting | bytes 2097152 | tf_op jit(solution)/shard_map/reshape | solution.py:150
  47.9 5.1 %all-to-all-start = ((f32[4,2,128,256]{3,2,1,0:T(8,128)}), f32[4,2,128,256]{3,2,1,0:T(8,128)S(1)}, u32[]{:S(2)}, u32[]{:S(2)}) async-start(f32[4,2,128,256]{3,2,1,0:T(8,128)} %bitcast.113), calls=%async_computation | async-start | bytes 2097152 | tf_op jit(solution)/shard_map/all_to_all | solution.py:151
  53.0 2.1 %fusion.23 = (f32[4,1,128,256]{2,3,1,0:T(8,128)S(1)}, f32[4,1,128,256]{2,3,1,0:T(8,128)}) fusion(f32[4,2,128,256]{2,3,1,0:T(8,128)} %copy-done.2), kind=kLoop, calls=%fused_computation.56 | loop fusion | bytes 2097152 | tf_op jit(solution)/shard_map/slice | solution.py:158
  55.5 2.1 %copy.48 = f32[4,1,128,256]{3,2,0,1:T(8,128)} copy(f32[4,1,128,256]{2,3,1,0:T(8,128)} %get-tuple-element.19) | data formatting | bytes 1048576
  57.6 1.1 slice_reduce_fusion
  58.7 2.3 %fusion.6 = f32[1,512,256]{1,2,0:T(8,128)} fusion(bf16[512,512]{1,0:T(8,128)(2,1)} %constant.86, f32[512,256]{1,0:T(8,128)} %bitcast.118, f32[32,8,4,128]{3,2,1,0:T(4,128)S(1)} %bitcast.112), kind=kOutput, calls=%fused_computation.18 | convolution fusion | flops 134348800 | bytes 2097152 | tf_op jit(solution)/shard_map/dot_general | solution.py:52
  61.0 17.2 %all-to-all-done = f32[4,2,128,256]{3,2,1,0:T(8,128)S(1)} async-done(((f32[4,2,128,256]{3,2,1,0:T(8,128)}), f32[4,2,128,256]{3,2,1,0:T(8,128)S(1)}, u32[]{:S(2)}, u32[]{:S(2)}) %all-to-all-start) | async-done | bytes 1048608 | tf_op jit(solution)/shard_map/all_to_all | solution.py:151
  78.9 1.4 copy-done.1
  83.0 1.1 bitcast_multiply_fusion.1
  85.2 1.3 fusion.9
  87.8 1.5 copy.51
  89.7 27.7 %all_to_all.15 = f32[4,2,128,256]{2,3,1,0:T(8,128)S(1)} all-to-all(f32[4,2,128,256]{2,3,1,0:T(8,128)S(1)} %broadcast_select_fusion), channel_id=1, replica_groups=mesh['groups'=2,'chan'=4,'win'=4] {'chan'}, dimensions={0} | all-to-all | bytes 2097152 | tf_op jit(solution)/shard_map/all_to_all | solution.py:172
  117.6 4.8 %fusion.27 = f32[128,2048]{1,0:T(8,128)S(1)} fusion(bf16[128,2048]{0,1:T(8,128)(2,1)S(1)} %get-tuple-element.13, bf16[2048,2048]{1,0:T(8,128)(2,1)} %constant.38.clone), kind=kOutput, calls=%fused_computation.60 | convolution fusion | flops 1073741824 | bytes 9961472 | tf_op jit(solution)/shard_map/dot_general | solution.py:52
  123.3 1.4 fusion.3
  124.8 1.1 reshape.156
  127.0 1.8 convolution_bitcast_fusion
  128.9 30.6 %reduce-scatter.3.cloned.1.call-done = f32[512,256]{0,1:T(8,128)} async-done(((f32[512,1024]{0,1:T(8,128)}), f32[512,256]{0,1:T(8,128)}) %reduce-scatter.3.cloned.1.call-update) | async-done | bytes 524304 | tf_op jit(solution)/shard_map/reduce_scatter | solution.py:182
  159.5 1.2 fusion.7
  160.7 22.8 %reduce-scatter.5.cloned.1.call-done = f32[128,256]{0,1:T(8,128)} async-done(((f32[512,256]{0,1:T(8,128)}), f32[128,256]{0,1:T(8,128)}) %reduce-scatter.5.cloned.1.call-update) | async-done | bytes 131088 | tf_op jit(solution)/shard_map/reduce_scatter | solution.py:183
  183.5 1.7 copy.47
  (54 shorter events, 10.6 us)
Async XLA Ops:
  7.2 12.8 %copy-start = (bf16[512,1024]{1,0:T(8,128)(2,1)S(1)}, bf16[512,1024]{1,0:T(8,128)(2,1)}, u32[]{:S(2)}) copy-start(bf16[512,1024]{1,0:T(8,128)(2,1)} %param.13) | copy-start | bytes 3145732
  10.8 7.5 %copy-start.7 = (s32[1,256]{1,0:T(1,128)S(1)}, s32[1,256]{1,0:T(1,128)}, u32[]{:S(2)}) copy-start(s32[1,256]{1,0:T(1,128)} %param.16) | copy-start | bytes 3076
  11.9 8.1 %copy-start.5 = (bf16[1,256,512]{2,1,0:T(8,128)(2,1)S(1)}, bf16[1,256,512]{2,1,0:T(8,128)(2,1)}, u32[]{:S(2)}) copy-start(bf16[1,256,512]{2,1,0:T(8,128)(2,1)} %param.12) | copy-start | bytes 786436
  11.9 35.0 %all-to-all-start.1 = ((f32[4,2,128,256]{2,3,1,0:T(8,128)}), f32[4,2,128,256]{2,3,1,0:T(8,128)S(1)}, u32[]{:S(2)}, u32[]{:S(2)}) async-start(f32[4,2,128,256]{2,3,1,0:T(8,128)} %maximum_bitcast_fusion), calls=%async_computation.1 | async-start | bytes 2097152 | tf_op jit(solution)/shard_map/all_to_all | solution.py:139
  46.9 1.0 copy-start.2
  47.9 30.3 %all-to-all-start = ((f32[4,2,128,256]{3,2,1,0:T(8,128)}), f32[4,2,128,256]{3,2,1,0:T(8,128)S(1)}, u32[]{:S(2)}, u32[]{:S(2)}) async-start(f32[4,2,128,256]{3,2,1,0:T(8,128)} %bitcast.113), calls=%async_computation | async-start | bytes 2097152 | tf_op jit(solution)/shard_map/all_to_all | solution.py:151
  53.0 106.5 %reduce-scatter.3.cloned.1.call-start = ((), (), s32[]{:S(2)}) async-start(), calls=%async_computation.5 | async-start | bytes 2621440 | tf_op jit(solution)/shard_map/reduce_scatter | solution.py:182
  78.7 1.6 copy-start.1
  81.4 1.6 copy-start.3
  83.0 1.1 copy-start.4
  117.4 5.0 %slice-start = ((s8[8388608]{0:T(1024)(128)(4,1)}), s8[4194304]{0:T(1024)(128)(4,1)S(1)}, s32[]{:S(2)}) async-start(s8[8388608]{0:T(1024)(128)(4,1)} %bitcast.105), calls=%async_computation.7 | async-start | bytes 8388608
  117.6 5.7 %slice-start.1 = ((s8[8388608]{0:T(1024)(128)(4,1)}), s8[4194304]{0:T(1024)(128)(4,1)S(1)}, s32[]{:S(2)}) async-start(s8[8388608]{0:T(1024)(128)(4,1)} %bitcast.105), calls=%async_computation.8 | async-start | bytes 8388608
  125.8 1.2 copy-start.6
  128.8 54.7 %reduce-scatter.5.cloned.1.call-start = ((), (), s32[]{:S(2)}) async-start(), calls=%async_computation.6 | async-start | bytes 655360 | tf_op jit(solution)/shard_map/reduce_scatter | solution.py:183
Sparse Core Ops, SparseCore 0:
  128.9 30.4 reduce-scatter.2
  161.8 21.6 reduce-scatter.4
where the time goes:
time: 193 us; the launch traced here: 192 us
  waiting for transfers between devices  70.6 us (37%)
  matrix products  32.4 us (17%)
  local copies, waits for them, and re-layouts  30.9 us (16%)
  blocking collectives  27.7 us (14%)
  between operations  14.4 us (7%)
  starting transfers between devices  11.6 us (6%)
  other arithmetic  4.47 us (2%)
    dot_general x13, matrix products, dot(): lax.dot_general(left, right, (dims, ((), ())), preferred_element_type=F32)  32.4 us
    reduce_scatter x1, waiting for transfers between devices, per_device(): lax.psum_scatter(grad_weight, 'win', scatter_dimension=1, tiled=True)  30.6 us
    all_to_all x1, blocking collectives, per_device(): lax.all_to_all(returned, 'chan', split_axis=0, concat_axis=0, tiled=True)  27.7 us
    reduce_scatter x1, waiting for transfers between devices, per_device(): lax.psum_scatter(grad_weight, 'chan', scatter_dimension=0, tiled=True)  22.8 us
    all_to_all x1, waiting for transfers between devices, per_device(): lax.all_to_all(spectrum, 'chan', split_axis=0, concat_axis=0, tiled=True)  17.2 us
    unnamed x27, local copies, waits for them, and re-layouts  9.65 us
    all_to_all x1, starting transfers between devices, per_device(): amp = lax.all_to_all(amp, 'chan', split_axis=0, concat_axis=0, tiled=True)  6.45 us
    reshape x2, local copies, waits for them, and re-layouts, per_device(): spectrum = spectrum.reshape(rows, blocks, 2, cols).transpose(1, 2, 0, 3)  5.63 us
  transfers between devices with their start and end apart: 4, of which 3 were waited for; matrix products, arithmetic and copies ran while one was open for 20% of the time, Pallas kernels for 0%

commit v1 on v0

--- a/solution.py
+++ b/solution.py
@@ -5,6 +5,8 @@
 import jax.numpy as jnp
 import numpy as np
 from jax import lax
+from jax.experimental import pallas as pl
+from jax.experimental.pallas import tpu as pltpu
 from jax.sharding import PartitionSpec as P
 
 PATCH_C = 16
@@ -110,12 +112,140 @@
 
 def chan_inverse(rows, channels, blocks):
     if channels <= DENSE_LIMIT:
-        high, _ = two_parts(chan_table(channels, blocks))
-        return dot(high, rows.astype(BF16), ((0,), (0,)))
+        high, low = two_parts(chan_table(channels, blocks))
+        rows_high, rows_low = split(rows)
+        back = ((0,), (0,))
+        return dot(high, rows_high, back) + dot(high, rows_low, back) + dot(low, rows_high, back)
     columns = rows.shape[1]
     shaped = factored_transform(rows.reshape(2, channels, columns), 1.0)
     shaped = shaped.reshape(2, blocks, channels // blocks, columns).transpose(1, 0, 2, 3)
     return shaped.reshape(2 * channels, columns)
+
+
+def time_forward_kernel(image_ref, high_ref, low_ref, out_ref):
+    image = image_ref[...]
+    rows = ((1,), (1,))
+    out_ref[0] = dot(image, high_ref[...], rows) + dot(image, low_ref[...], rows)
+
+
+def time_forward(image, high, low, cols):
+    rows, samples = image.shape
+    steps = samples // cols
+    return pl.pallas_call(
+        time_forward_kernel,
+        grid=(steps,),
+        in_specs=[
+            pl.BlockSpec((rows, samples), lambda i: (0, 0)),
+            pl.BlockSpec((cols, samples), lambda i: (i, 0)),
+            pl.BlockSpec((cols, samples), lambda i: (i, 0)),
+        ],
+        out_specs=pl.BlockSpec((1, rows, cols), lambda i: (i, 0, 0)),
+        out_shape=jax.ShapeDtypeStruct((steps, rows, cols), F32),
+        cost_estimate=pl.CostEstimate(
+            flops=4 * rows * samples * samples, bytes_accessed=4 * samples * samples, transcendentals=0
+        ),
+        compiler_params=pltpu.CompilerParams(vmem_limit_bytes=32 * 1024 * 1024),
+    )(image, high, low)
+
+
+def reduce_kernel(
+    part_ref, out_ref, from_core, pair_sum, from_chip, win_sum, from_chan,
+    core_send, core_recv, chip_send, chip_recv, chan_send, chan_recv,
+):
+    chan = lax.axis_index("chan")
+    win = lax.axis_index("win")
+    core = lax.rem(win, 2)
+    chip = win // 2
+    cols = out_ref.shape[1]
+    core_peer = chip * 2 + 1 - core
+    chip_peer = (1 - chip) * 2 + core
+    barrier = pltpu.get_barrier_semaphore()
+    mesh_ids = pl.DeviceIdType.MESH
+    for peer in (core_peer, chip_peer):
+        pl.semaphore_signal(barrier, inc=1, device_id={"win": peer}, device_id_type=mesh_ids)
+    for step in range(1, 4):
+        pl.semaphore_signal(barrier, inc=1, device_id={"chan": lax.rem(chan + step, 4)}, device_id_type=mesh_ids)
+    pl.semaphore_wait(barrier, 5)
+
+    def block(index):
+        return pl.ds(pl.multiple_of(index * cols, 128), cols)
+
+    core_copies = []
+    for step in range(4):
+        row = lax.rem(chan + 1 + step, 4)
+        for side in range(2):
+            copy = pltpu.make_async_remote_copy(
+                src_ref=part_ref.at[row, :, block(2 * side + 1 - core)],
+                dst_ref=from_core.at[step, side],
+                send_sem=core_send.at[step, side],
+                recv_sem=core_recv.at[step, side],
+                device_id={"win": core_peer},
+                device_id_type=mesh_ids,
+            )
+            copy.start()
+            core_copies.append(copy)
+    chip_copies = []
+    for step in range(4):
+        row = lax.rem(chan + 1 + step, 4)
+        for side in range(2):
+            core_copies[2 * step + side].wait()
+            pair_sum[step, side] = part_ref[row, :, block(2 * side + core)] + from_core[step, side]
+        copy = pltpu.make_async_remote_copy(
+            src_ref=pair_sum.at[step, 1 - chip],
+            dst_ref=from_chip.at[step],
+            send_sem=chip_send.at[step],
+            recv_sem=chip_recv.at[step],
+            device_id={"win": chip_peer},
+            device_id_type=mesh_ids,
+        )
+        copy.start()
+        chip_copies.append(copy)
+    chan_copies = []
+    for step in range(4):
+        chip_copies[step].wait()
+        win_sum[step] = pair_sum[step, chip] + from_chip[step]
+        if step < 3:
+            copy = pltpu.make_async_remote_copy(
+                src_ref=win_sum.at[step],
+                dst_ref=from_chan.at[step],
+                send_sem=chan_send.at[step],
+                recv_sem=chan_recv.at[step],
+                device_id={"chan": lax.rem(chan + 1 + step, 4)},
+                device_id_type=mesh_ids,
+            )
+            copy.start()
+            chan_copies.append(copy)
+    for copy in chan_copies:
+        copy.wait()
+    out_ref[...] = win_sum[3] + from_chan[0] + from_chan[1] + from_chan[2]
+
+
+def reduce_scatter(part):
+    rows, columns = part.shape[0] // 4, part.shape[1] // 4
+    piece = (rows, columns)
+    dma = pltpu.SemaphoreType.DMA
+    return pl.pallas_call(
+        reduce_kernel,
+        in_specs=[pl.BlockSpec(memory_space=pltpu.VMEM)],
+        out_specs=pl.BlockSpec(memory_space=pltpu.VMEM),
+        out_shape=jax.ShapeDtypeStruct(piece, F32),
+        scratch_shapes=[
+            pltpu.VMEM((4, 2) + piece, F32),
+            pltpu.VMEM((4, 2) + piece, F32),
+            pltpu.VMEM((4,) + piece, F32),
+            pltpu.VMEM((4,) + piece, F32),
+            pltpu.VMEM((3,) + piece, F32),
+            dma((4, 2)),
+            dma((4, 2)),
+            dma((4,)),
+            dma((4,)),
+            dma((3,)),
+            dma((3,)),
+        ],
+        compiler_params=pltpu.CompilerParams(
+            collective_id=0, has_side_effects=True, vmem_limit_bytes=32 * 1024 * 1024
+        ),
+    )(part.reshape((4, rows, 4 * columns)))
 
 
 def per_device(tokens, head_weight, target, target_amp, patch_ranks):
@@ -146,8 +276,7 @@
     composite = jnp.where(pixel_mask, image, target)
 
     high, low = two_parts(time_table(samples, blocks))
-    spectrum = dot(composite, high, ((1,), (1,))) + dot(composite, low, ((1,), (1,)))
-    spectrum = spectrum.reshape(rows, blocks, 2, cols).transpose(1, 2, 0, 3)
+    spectrum = time_forward(composite, high, low, cols).reshape(blocks, 2, rows, cols)
     spectrum = lax.all_to_all(spectrum, "chan", split_axis=0, concat_axis=0, tiled=True)
 
     lane = lax.broadcasted_iota(jnp.int32, (1, 128), 1)
@@ -179,8 +308,11 @@
     grad_patches = grad_patches.transpose(0, 2, 1, 3).reshape(local_patches, PATCH_C * PATCH_S)
     grad_tokens = dot(grad_patches, head_weight, ((1,), (1,))).astype(BF16)
     grad_weight = dot(tokens, grad_patches, ((0,), (0,)))
-    grad_weight = lax.psum_scatter(grad_weight, "win", scatter_dimension=1, tiled=True)
-    grad_weight = lax.psum_scatter(grad_weight, "chan", scatter_dimension=0, tiled=True)
+    if all_windows == 4 and blocks == 4:
+        grad_weight = reduce_scatter(grad_weight)
+    else:
+        grad_weight = lax.psum_scatter(grad_weight, "win", scatter_dimension=1, tiled=True)
+        grad_weight = lax.psum_scatter(grad_weight, "chan", scatter_dimension=0, tiled=True)
     return (grad_tokens[None], grad_weight)
 
 

time: 193 us -> 166 us (0.86)
  waiting for transfers between devices: 70.6 us -> 38.8 us
  Pallas kernels: 0 us -> 28.2 us
  between operations: 14.4 us -> 1.01 us
  matrix products: 32.4 us -> 23.8 us
    reduce_scatter x2 -> x0, waiting for transfers between devices: 53.4 us -> none  [the longest x1 30.6 us: per_device(): lax.psum_scatter(grad_weight, 'win', scatter_dimension=1, tiled=True)]
    pallas_call x0 -> x2, Pallas kernels: none -> 28.2 us  [the longest x1 20.8 us: reduce_scatter(): pl.pallas_call(reduce_kernel, in_specs=[pl.BlockSpec(memory_space=pltpu.V...]
    all_to_all x1, waiting for transfers between devices: 0.01 us -> 18.5 us  [per_device(): amp = lax.all_to_all(amp, 'chan', split_axis=0, concat_axis=0, tiled=True)]
    dot_general x13, matrix products: 32.4 us -> 23.8 us  [dot(): lax.dot_general(left, right, (dims, ((), ())), preferred_element_type=F32)]
    reshape x2 -> x1, local copies, waits for them, and re-layouts: 5.63 us -> 2.51 us  [per_device(): back = back.reshape(blocks, 2, rows, cols + 128)]
    all_to_all x1, waiting for transfers between devices: 17.2 us -> 20.2 us  [per_device(): lax.all_to_all(spectrum, 'chan', split_axis=0, concat_axis=0, tiled=True)]
    unnamed x27 -> x30, local copies, waits for them, and re-layouts: 9.65 us -> 12.6 us
    transpose x1 -> x0, local copies, waits for them, and re-layouts: 2.48 us -> none  [per_device(): image = image.transpose(0, 2, 1, 3).reshape(rows, samples)]
  transfers between devices with their start and end apart: 4 -> 2, of which waited for: 3 -> 2; matrix products, arithmetic and copies ran while one was open for 20% -> 6% of each run, Pallas kernels for 0% -> 0%
where the time goes in v1:
time: 166 us; the launch traced here: 165 us
  waiting for transfers between devices  38.8 us (23%)
  local copies, waits for them, and re-layouts  30.6 us (18%)
  Pallas kernels  28.2 us (17%)
  blocking collectives  27.7 us (17%)
  matrix products  23.8 us (14%)
  starting transfers between devices  10.7 us (6%)
  other arithmetic  4.21 us (3%)
    all_to_all x1, blocking collectives, per_device(): lax.all_to_all(returned, 'chan', split_axis=0, concat_axis=0, tiled=True)  27.7 us
    dot_general x13, matrix products, dot(): lax.dot_general(left, right, (dims, ((), ())), preferred_element_type=F32)  23.8 us
    pallas_call x1, Pallas kernels, reduce_scatter(): pl.pallas_call(reduce_kernel, in_specs=[pl.BlockSpec(memory_space=pltpu.V...  20.8 us
    all_to_all x1, waiting for transfers between devices, per_device(): lax.all_to_all(spectrum, 'chan', split_axis=0, concat_axis=0, tiled=True)  20.2 us
    all_to_all x1, waiting for transfers between devices, per_device(): amp = lax.all_to_all(amp, 'chan', split_axis=0, concat_axis=0, tiled=True)  18.5 us
    unnamed x30, local copies, waits for them, and re-layouts  12.6 us
    pallas_call x1, Pallas kernels, time_forward(): pl.pallas_call(time_forward_kernel, grid=(steps,), in_specs=[pl.BlockSpec...  7.39 us
    all_to_all x1, starting transfers between devices, per_device(): lax.all_to_all(spectrum, 'chan', split_axis=0, concat_axis=0, tiled=True)  6.31 us
  transfers between devices with their start and end apart: 2, of which 2 were waited for; matrix products, arithmetic and copies ran while one was open for 6% of the time, Pallas kernels for 0%

profile of v1, /device:TPU:0, one launch (start us, length us, event | category | flops | bytes accessed | tf_op | source)
XLA Modules:
  0.0 165.0 jit_solution(8596976773185100533)
XLA Ops:
  1.7 1.3 reshape.152
  3.0 1.5 convolution_convert_fusion
  5.2 1.2 copy.53
  6.4 2.0 %reshape.154 = bf16[128,2048]{1,0:T(8,128)(2,1)S(1)} reshape(bf16[8,16,32,64]{3,2,1,0:T(8,128)(2,1)} %bitcast.123) | data formatting | bytes 1048576 | tf_op jit(solution)/shard_map/reshape | solution.py:273
  8.6 3.4 %copy-done.1 = bf16[2048,2048]{1,0:T(8,128)(2,1)S(1)} copy-done((bf16[2048,2048]{1,0:T(8,128)(2,1)S(1)}, bf16[2048,2048]{1,0:T(8,128)(2,1)}, u32[]{:S(2)}) %copy-start.1) | copy-done | bytes 8388632
  12.0 3.4 %copy-done.2 = bf16[2048,2048]{1,0:T(8,128)(2,1)S(1)} copy-done((bf16[2048,2048]{1,0:T(8,128)(2,1)S(1)}, bf16[2048,2048]{1,0:T(8,128)(2,1)}, u32[]{:S(2)}) %copy-start.2) | copy-done | bytes 8388632
  15.4 7.4 %shard_map.140 = f32[8,128,256]{2,1,0:T(8,128)} custom-call(bf16[128,2048]{1,0:T(8,128)(2,1)S(1)} %bitcast_select_fusion.image_ref, bf16[2048,2048]{1,0:T(8,128)(2,1)S(1)} %copy-done.1, bf16[2048,2048]{1,0:T(8,128)(2,1)S(1)} %copy-done.2), custom_call_target="tpu_custom_call" | custom-call | flops 2147483648 | bytes 16777216 | tf_op jit(solution)/shard_map/pallas_call | solution.py:134
  22.8 6.3 %all-to-all-start = ((f32[4,2,128,256]{3,2,1,0:T(8,128)}), f32[4,2,128,256]{3,2,1,0:T(8,128)S(1)}, u32[]{:S(2)}, u32[]{:S(2)}) async-start(f32[4,2,128,256]{3,2,1,0:T(8,128)} %bitcast.3), calls=%async_computation | async-start | bytes 2097152 | tf_op jit(solution)/shard_map/all_to_all | solution.py:280
  31.1 2.4 %fusion.20 = f32[1024,128]{1,0:T(8,128)S(1)} fusion(bf16[1024,1024]{1,0:T(8,128)(2,1)} %constant.37.clone, bf16[128,2048]{1,0:T(8,128)(2,1)} %bitcast.131), kind=kOutput, calls=%fused_computation.48 | convolution fusion | flops 268435456 | bytes 2883584 | tf_op jit(solution)/shard_map/dot_general | solution.py:54
  33.5 1.1 maximum_bitcast_fusion
  34.6 20.2 %all-to-all-done = f32[4,2,128,256]{3,2,1,0:T(8,128)S(1)} async-done(((f32[4,2,128,256]{3,2,1,0:T(8,128)}), f32[4,2,128,256]{3,2,1,0:T(8,128)S(1)}, u32[]{:S(2)}, u32[]{:S(2)}) %all-to-all-start) | async-done | bytes 1048608 | tf_op jit(solution)/shard_map/all_to_all | solution.py:280
  54.8 4.4 %all-to-all-start.1 = ((f32[4,2,128,256]{2,3,1,0:T(8,128)}), f32[4,2,128,256]{2,3,1,0:T(8,128)}, u32[]{:S(2)}, u32[]{:S(2)}) async-start(f32[4,2,128,256]{2,3,1,0:T(8,128)} %maximum_bitcast_fusion), calls=%async_computation.1 | async-start | bytes 2097152 | tf_op jit(solution)/shard_map/all_to_all | solution.py:269
  60.0 1.4 copy-done.3
  61.4 2.2 %fusion.28 = f32[384,1024]{1,0:T(8,128)} fusion(bf16[1024,384]{1,0:T(8,128)(2,1)S(1)} %get-tuple-element.7, bf16[1024,1024]{1,0:T(8,128)(2,1)S(1)} %copy-done.3), kind=kOutput, calls=%fused_computation.59 | convolution fusion | flops 805306368 | bytes 4456448 | tf_op jit(solution)/shard_map/dot_general | solution.py:54
  63.7 2.2 %fusion.29 = f32[384,1024]{1,0:T(8,128)} fusion(bf16[1024,384]{1,0:T(8,128)(2,1)S(1)} %get-tuple-element.6, bf16[1024,1024]{1,0:T(8,128)(2,1)S(1)} %copy-done.3), kind=kOutput, calls=%fused_computation.60 | convolution fusion | flops 805306368 | bytes 4456448 | tf_op jit(solution)/shard_map/dot_general | solution.py:54
  65.8 18.5 %all-to-all-done.1 = f32[4,2,128,256]{2,3,1,0:T(8,128)} async-done(((f32[4,2,128,256]{2,3,1,0:T(8,128)}), f32[4,2,128,256]{2,3,1,0:T(8,128)}, u32[]{:S(2)}, u32[]{:S(2)}) %all-to-all-start.1) | async-done | bytes 1048608 | tf_op jit(solution)/shard_map/all_to_all | solution.py:269
  84.4 2.1 %fusion.27 = (f32[4,1,128,256]{2,3,1,0:T(8,128)S(1)}, f32[4,1,128,256]{2,3,1,0:T(8,128)}) fusion(f32[4,2,128,256]{2,3,1,0:T(8,128)} %all-to-all-done.1), kind=kLoop, calls=%fused_computation.58 | loop fusion | bytes 2097152 | tf_op jit(solution)/shard_map/slice | solution.py:287
  86.9 1.2 copy.42
  88.3 1.5 fusion.5
  89.9 2.9 %bitcast_multiply_fusion.1 = (f32[1024,384]{0,1:T(8,128)S(1)}, f32[384,1024]{1,0:T(8,128)S(1)}) fusion(bf16[1024,384]{1,0:T(8,128)(2,1)S(1)} %get-tuple-element.7, bf16[1024,1024]{1,0:T(8,128)(2,1)S(1)} %copy-done.5, f32[384,1024]{1,0:T(8,128)} %fusion.28, f32[384,1024]{1,0:T(8,128)} %fusion.29), kind=kOutput, calls=%fused_computation.8 | convolution fusion | flops 806486016 | bytes 9175040 | tf_op jit(solution)/shard_map/dot_general | solution.py:54
  94.0 1.2 copy-done.4
  95.2 1.1 fusion.8
  96.3 1.0 fusion.24
  98.4 2.5 %reshape.157 = f32[4,2,128,384]{2,1,0,3:T(2,128)} reshape(f32[1024,384]{0,1:T(8,128)S(1)} %add_bitcast_fusion) | data formatting | bytes 3145728 | tf_op jit(solution)/shard_map/reshape | solution.py:297
  102.4 27.7 %all_to_all.15 = f32[4,2,128,256]{2,3,1,0:T(8,128)S(1)} all-to-all(f32[4,2,128,256]{2,3,1,0:T(8,128)S(1)} %copy_select_fusion), channel_id=1, replica_groups=mesh['groups'=2,'chan'=4,'win'=4] {'chan'}, dimensions={0} | all-to-all | bytes 2097152 | tf_op jit(solution)/shard_map/all_to_all | solution.py:301
  130.3 4.8 %fusion.30 = f32[128,2048]{1,0:T(8,128)S(1)} fusion(bf16[128,2048]{0,1:T(8,128)(2,1)S(1)} %get-tuple-element.5, bf16[2048,2048]{1,0:T(8,128)(2,1)} %constant.38.clone.high_ref), kind=kOutput, calls=%fused_computation.61 | convolution fusion | flops 1073741824 | bytes 9961472 | tf_op jit(solution)/shard_map/dot_general | solution.py:54
  136.0 1.4 fusion.3
  137.4 1.1 reshape.159
  138.5 1.4 copy.52
  139.9 1.9 %reshape.160 = bf16[256,1024]{1,0:T(8,128)(2,1)S(1)} reshape(bf16[8,32,16,64]{3,2,1,0:T(8,128)(2,1)} %bitcast.124) | data formatting | bytes 1048576 | tf_op jit(solution)/shard_map/reshape | solution.py:308
  142.3 1.2 fusion.6
  143.5 20.8 %shard_map.141 = f32[128,256]{1,0:T(8,128)S(1)} custom-call(f32[4,128,1024]{2,1,0:T(8,128)S(1)} %bitcast.116), custom_call_target="tpu_custom_call" | custom-call | tf_op jit(solution)/shard_map/pallas_call | solution.py:227
  (53 shorter events, 11.1 us)
Async XLA Ops:
  0.6 2.4 %copy-start = (bf16[512,1024]{1,0:T(8,128)(2,1)S(1)}, bf16[512,1024]{1,0:T(8,128)(2,1)}, u32[]{:S(2)}) copy-start(bf16[512,1024]{1,0:T(8,128)(2,1)} %param.14) | copy-start | bytes 3145732
  3.0 5.5 %copy-start.6 = (pred[128,2048]{1,0:T(32,128)(4,1)}, pred[128,2048]{1,0:T(32,128)(4,1)S(1)}, u32[]{:S(2)}) copy-start(pred[128,2048]{1,0:T(32,128)(4,1)S(1)} %reshape.152) | copy-start | bytes 786436
  5.2 3.3 %copy-start.10 = (bf16[1,128,2048]{2,1,0:T(8,128)(2,1)S(1)}, bf16[1,128,2048]{2,1,0:T(8,128)(2,1)}, u32[]{:S(2)}) copy-start(bf16[1,128,2048]{2,1,0:T(8,128)(2,1)} %param.15) | copy-start | bytes 1572868
  8.6 3.4 %copy-start.1 = (bf16[2048,2048]{1,0:T(8,128)(2,1)S(1)}, bf16[2048,2048]{1,0:T(8,128)(2,1)}, u32[]{:S(2)}) copy-start(bf16[2048,2048]{1,0:T(8,128)(2,1)} %constant.38.clone.high_ref) | copy-start | bytes 25165828
  12.0 3.4 %copy-start.2 = (bf16[2048,2048]{1,0:T(8,128)(2,1)S(1)}, bf16[2048,2048]{1,0:T(8,128)(2,1)}, u32[]{:S(2)}) copy-start(bf16[2048,2048]{1,0:T(8,128)(2,1)} %constant.39.clone.low_ref) | copy-start | bytes 25165828
  22.8 32.0 %all-to-all-start = ((f32[4,2,128,256]{3,2,1,0:T(8,128)}), f32[4,2,128,256]{3,2,1,0:T(8,128)S(1)}, u32[]{:S(2)}, u32[]{:S(2)}) async-start(f32[4,2,128,256]{3,2,1,0:T(8,128)} %bitcast.3), calls=%async_computation | async-start | bytes 2097152 | tf_op jit(solution)/shard_map/all_to_all | solution.py:280
  31.1 2.4 %copy-start.8 = (f32[128,1024]{0,1:T(8,128)S(1)}, f32[128,1024]{0,1:T(8,128)}, u32[]{:S(2)}) copy-start(f32[128,1024]{0,1:T(8,128)} %copy.36) | copy-start | bytes 1572868
  54.8 29.5 %all-to-all-start.1 = ((f32[4,2,128,256]{2,3,1,0:T(8,128)}), f32[4,2,128,256]{2,3,1,0:T(8,128)}, u32[]{:S(2)}, u32[]{:S(2)}) async-start(f32[4,2,128,256]{2,3,1,0:T(8,128)} %maximum_bitcast_fusion), calls=%async_computation.1 | async-start | bytes 2097152 | tf_op jit(solution)/shard_map/all_to_all | solution.py:269
  59.8 1.6 copy-start.3
  88.1 1.8 %copy-start.5 = (bf16[1024,1024]{1,0:T(8,128)(2,1)S(1)}, bf16[1024,1024]{1,0:T(8,128)(2,1)}, u32[]{:S(2)}) copy-start(bf16[1024,1024]{1,0:T(8,128)(2,1)} %constant.42.clone) | copy-start | bytes 6291460
  93.7 1.6 copy-start.4
  100.9 1.2 slice-start.2
  130.1 5.0 %slice-start = ((s8[8388608]{0:T(1024)(128)(4,1)}), s8[4194304]{0:T(1024)(128)(4,1)S(1)}, s32[]{:S(2)}) async-start(s8[8388608]{0:T(1024)(128)(4,1)} %bitcast.114), calls=%async_computation.3 | async-start | bytes 8388608
  130.2 5.7 %slice-start.1 = ((s8[8388608]{0:T(1024)(128)(4,1)}), s8[4194304]{0:T(1024)(128)(4,1)S(1)}, s32[]{:S(2)}) async-start(s8[8388608]{0:T(1024)(128)(4,1)} %bitcast.114), calls=%async_computation.4 | async-start | bytes 8388608
  130.2 5.7 %copy-start.7 = (pred[128,2048]{1,0:T(32,128)(4,1)S(1)}, pred[128,2048]{1,0:T(32,128)(4,1)}, u32[]{:S(2)}) copy-start(pred[128,2048]{1,0:T(32,128)(4,1)} %copy-done.6) | copy-start | bytes 786436
  138.5 3.4 %copy-start.9 = (bf16[1,256,512]{2,1,0:T(8,128)(2,1)S(1)}, bf16[1,256,512]{2,1,0:T(8,128)(2,1)}, u32[]{:S(2)}) copy-start(bf16[1,256,512]{2,1,0:T(8,128)(2,1)} %param.13) | copy-start | bytes 786436

commit v2 on v1

--- a/solution.py
+++ b/solution.py
@@ -277,6 +277,7 @@
 
     high, low = two_parts(time_table(samples, blocks))
     spectrum = time_forward(composite, high, low, cols).reshape(blocks, 2, rows, cols)
+    spectrum, amp = lax.optimization_barrier((spectrum, amp))
     spectrum = lax.all_to_all(spectrum, "chan", split_axis=0, concat_axis=0, tiled=True)
 
     lane = lax.broadcasted_iota(jnp.int32, (1, 128), 1)

time: 166 us -> 146 us (0.88)
  waiting for transfers between devices: 38.8 us -> 24 us
  matrix products: 23.8 us -> 16.6 us
  local copies, waits for them, and re-layouts: 30.6 us -> 33 us
    all_to_all x1, waiting for transfers between devices: 18.5 us -> 2.18 us  [per_device(): amp = lax.all_to_all(amp, 'chan', split_axis=0, concat_axis=0, tiled=True)]
    dot_general x13, matrix products: 23.8 us -> 16.6 us  [dot(): lax.dot_general(left, right, (dims, ((), ())), preferred_element_type=F32)]
    reshape x2, local copies, waits for them, and re-layouts: 1.9 us -> 4.12 us  [per_device(): image = patches.reshape(chan_patches, sample_patches, PATCH_C, PATCH_S)]
    slice x2, local copies, waits for them, and re-layouts: 2.42 us -> 0.38 us  [per_device(): amp_low = amp[:, 0].reshape(channels, cols)]
    all_to_all x1, starting transfers between devices: 4.43 us -> 6.45 us  [per_device(): amp = lax.all_to_all(amp, 'chan', split_axis=0, concat_axis=0, tiled=True)]
    all_to_all x1, starting transfers between devices: 6.31 us -> 4.42 us  [per_device(): lax.all_to_all(spectrum, 'chan', split_axis=0, concat_axis=0, tiled=True)]
  transfers between devices with their start and end apart: 2 -> 2, of which waited for: 2 -> 2; matrix products, arithmetic and copies ran while one was open for 6% -> 8% of each run, Pallas kernels for 0% -> 5%
where the time goes in v2:
time: 146 us; the launch traced here: 145 us
  local copies, waits for them, and re-layouts  33 us (23%)
  Pallas kernels  28.2 us (19%)
  blocking collectives  27.7 us (19%)
  waiting for transfers between devices  24 us (16%)
  matrix products  16.6 us (11%)
  starting transfers between devices  10.9 us (7%)
  other arithmetic  3.78 us (3%)
    all_to_all x1, blocking collectives, per_device(): lax.all_to_all(returned, 'chan', split_axis=0, concat_axis=0, tiled=True)  27.7 us
    all_to_all x1, waiting for transfers between devices, per_device(): lax.all_to_all(spectrum, 'chan', split_axis=0, concat_axis=0, tiled=True)  21.9 us
    pallas_call x1, Pallas kernels, reduce_scatter(): pl.pallas_call(reduce_kernel, in_specs=[pl.BlockSpec(memory_space=pltpu.V...  20.8 us
    dot_general x13, matrix products, dot(): lax.dot_general(left, right, (dims, ((), ())), preferred_element_type=F32)  16.6 us
    unnamed x30, local copies, waits for them, and re-layouts  13.7 us
    pallas_call x1, Pallas kernels, time_forward(): pl.pallas_call(time_forward_kernel, grid=(steps,), in_specs=[pl.BlockSpec...  7.38 us
    all_to_all x1, starting transfers between devices, per_device(): amp = lax.all_to_all(amp, 'chan', split_axis=0, concat_axis=0, tiled=True)  6.45 us
    all_to_all x1, starting transfers between devices, per_device(): lax.all_to_all(spectrum, 'chan', split_axis=0, concat_axis=0, tiled=True)  4.42 us
  transfers between devices with their start and end apart: 2, of which 2 were waited for; matrix products, arithmetic and copies ran while one was open for 8% of the time, Pallas kernels for 5%

profile of v2, /device:TPU:0, one launch (start us, length us, event | category | flops | bytes accessed | tf_op | source)
XLA Modules:
  0.0 145.2 jit_solution(4269893774976004808)
XLA Ops:
  0.7 2.2 %copy.31 = bf16[1,128,2048]{1,2,0:T(8,128)(2,1)} copy(bf16[1,128,2048]{2,1,0:T(8,128)(2,1)} %param.16) | data formatting | bytes 1048576 | tf_op args[3]
  3.9 1.7 %fusion.20 = f32[1024,128]{1,0:T(8,128)S(1)} fusion(bf16[1024,1024]{1,0:T(8,128)(2,1)S(1)} %copy-done.5, bf16[128,2048]{0,1:T(8,128)(2,1)} %bitcast.128), kind=kOutput, calls=%fused_computation.47 | convolution fusion | flops 268435456 | bytes 2883584 | tf_op jit(solution)/shard_map/dot_general | solution.py:54
  5.6 1.0 copy.32
  6.7 6.5 %all-to-all-start = ((f32[4,2,128,256]{2,3,1,0:T(8,128)}), f32[4,2,128,256]{2,3,1,0:T(8,128)S(1)}, u32[]{:S(2)}, u32[]{:S(2)}) async-start(f32[4,2,128,256]{2,3,1,0:T(8,128)} %copy.32), calls=%async_computation | async-start | bytes 2097152 | tf_op jit(solution)/shard_map/all_to_all | solution.py:269
  13.5 1.3 reshape.152
  15.2 1.7 %reshape.153 = bf16[8,32,16,64]{3,2,1,0:T(8,128)(2,1)} reshape(bf16[256,1024]{1,0:T(8,128)(2,1)S(1)} %convolution_convert_fusion) | data formatting | bytes 1048576 | tf_op jit(solution)/shard_map/reshape | solution.py:272
  16.9 2.5 %copy.47 = bf16[8,32,16,64]{3,1,2,0:T(8,128)(2,1)} copy(bf16[8,32,16,64]{3,2,1,0:T(8,128)(2,1)} %reshape.153) | data formatting | bytes 1048576 | tf_op jit(solution)/shard_map/reshape | solution.py:272
  19.3 2.0 %reshape.154 = bf16[128,2048]{1,0:T(8,128)(2,1)S(1)} reshape(bf16[8,16,32,64]{3,2,1,0:T(8,128)(2,1)} %bitcast.122) | data formatting | bytes 1048576 | tf_op jit(solution)/shard_map/reshape | solution.py:273
  21.4 1.2 bitcast_select_fusion.image_ref
  22.6 3.4 %copy-done.1 = bf16[2048,2048]{1,0:T(8,128)(2,1)S(1)} copy-done((bf16[2048,2048]{1,0:T(8,128)(2,1)S(1)}, bf16[2048,2048]{1,0:T(8,128)(2,1)}, u32[]{:S(2)}) %copy-start.1) | copy-done | bytes 8388632
  25.9 3.4 %copy-done.2 = bf16[2048,2048]{1,0:T(8,128)(2,1)S(1)} copy-done((bf16[2048,2048]{1,0:T(8,128)(2,1)S(1)}, bf16[2048,2048]{1,0:T(8,128)(2,1)}, u32[]{:S(2)}) %copy-start.2) | copy-done | bytes 8388632
  29.3 7.4 %shard_map.140 = f32[8,128,256]{2,1,0:T(8,128)} custom-call(bf16[128,2048]{1,0:T(8,128)(2,1)S(1)} %bitcast_select_fusion.image_ref, bf16[2048,2048]{1,0:T(8,128)(2,1)S(1)} %copy-done.1, bf16[2048,2048]{1,0:T(8,128)(2,1)S(1)} %copy-done.2), custom_call_target="tpu_custom_call" | custom-call | flops 2147483648 | bytes 16777216 | tf_op jit(solution)/shard_map/pallas_call | solution.py:134
  36.7 2.2 %all-to-all-done = f32[4,2,128,256]{2,3,1,0:T(8,128)S(1)} async-done(((f32[4,2,128,256]{2,3,1,0:T(8,128)}), f32[4,2,128,256]{2,3,1,0:T(8,128)S(1)}, u32[]{:S(2)}, u32[]{:S(2)}) %all-to-all-start) | async-done | bytes 1048608 | tf_op jit(solution)/shard_map/all_to_all | solution.py:269
  38.9 4.4 %all-to-all-start.1 = ((f32[4,2,128,256]{3,2,1,0:T(8,128)}), f32[4,2,128,256]{3,2,1,0:T(8,128)}, u32[]{:S(2)}, u32[]{:S(2)}) async-start(f32[4,2,128,256]{3,2,1,0:T(8,128)} %bitcast.3), calls=%async_computation.1 | async-start | bytes 2097152 | tf_op jit(solution)/shard_map/all_to_all | solution.py:281
  43.4 1.3 copy.34
  46.6 21.9 %all-to-all-done.1 = f32[4,2,128,256]{3,2,1,0:T(8,128)} async-done(((f32[4,2,128,256]{3,2,1,0:T(8,128)}), f32[4,2,128,256]{3,2,1,0:T(8,128)}, u32[]{:S(2)}, u32[]{:S(2)}) %all-to-all-start.1) | async-done | bytes 1048608 | tf_op jit(solution)/shard_map/all_to_all | solution.py:281
  68.4 1.2 slice_reduce_fusion.2
  69.9 1.3 select_maximum_fusion
  71.4 1.4 copy-done.4
  72.8 1.0 fusion.27
  73.9 1.0 fusion.28
  75.5 1.1 bitcast_multiply_fusion.1
  77.7 1.0 fusion.8
  78.7 1.0 fusion.24
  79.7 1.0 add_bitcast_fusion
  80.8 2.5 %reshape.157 = f32[4,2,128,384]{2,1,0,3:T(2,128)} reshape(f32[1024,384]{0,1:T(8,128)S(1)} %add_bitcast_fusion) | data formatting | bytes 3145728 | tf_op jit(solution)/shard_map/reshape | solution.py:298
  84.8 27.7 %all_to_all.15 = f32[4,2,128,256]{2,3,1,0:T(8,128)S(1)} all-to-all(f32[4,2,128,256]{2,3,1,0:T(8,128)S(1)} %copy_select_fusion), channel_id=1, replica_groups=mesh['groups'=2,'chan'=4,'win'=4] {'chan'}, dimensions={0} | all-to-all | bytes 2097152 | tf_op jit(solution)/shard_map/all_to_all | solution.py:302
  112.6 4.8 %fusion.29 = f32[128,2048]{1,0:T(8,128)S(1)} fusion(bf16[128,2048]{0,1:T(8,128)(2,1)S(1)} %get-tuple-element.9, bf16[2048,2048]{1,0:T(8,128)(2,1)} %constant.38.clone.high_ref), kind=kOutput, calls=%fused_computation.59 | convolution fusion | flops 1073741824 | bytes 9961472 | tf_op jit(solution)/shard_map/dot_general | solution.py:54
  118.4 1.4 fusion.3
  119.8 1.1 reshape.159
  122.5 1.2 fusion.6
  123.7 20.8 %shard_map.141 = f32[128,256]{1,0:T(8,128)S(1)} custom-call(f32[4,128,1024]{2,1,0:T(8,128)S(1)} %bitcast.115), custom_call_target="tpu_custom_call" | custom-call | tf_op jit(solution)/shard_map/pallas_call | solution.py:227
  (56 shorter events, 10.6 us)
Async XLA Ops:
  0.6 14.1 %copy-start = (bf16[512,1024]{1,0:T(8,128)(2,1)S(1)}, bf16[512,1024]{1,0:T(8,128)(2,1)}, u32[]{:S(2)}) copy-start(bf16[512,1024]{1,0:T(8,128)(2,1)} %param.14) | copy-start | bytes 3145732
  0.6 3.2 %copy-start.5 = (bf16[1024,1024]{1,0:T(8,128)(2,1)S(1)}, bf16[1024,1024]{1,0:T(8,128)(2,1)}, u32[]{:S(2)}) copy-start(bf16[1024,1024]{1,0:T(8,128)(2,1)} %constant.37.clone) | copy-start | bytes 6291460
  5.6 7.5 %copy-start.10 = (s32[1,256]{1,0:T(1,128)S(1)}, s32[1,256]{1,0:T(1,128)}, u32[]{:S(2)}) copy-start(s32[1,256]{1,0:T(1,128)} %param.17) | copy-start | bytes 3076
  6.7 8.1 %copy-start.7 = (bf16[1,256,512]{2,1,0:T(8,128)(2,1)S(1)}, bf16[1,256,512]{2,1,0:T(8,128)(2,1)}, u32[]{:S(2)}) copy-start(bf16[1,256,512]{2,1,0:T(8,128)(2,1)} %param.13) | copy-start | bytes 786436
  6.7 32.2 %all-to-all-start = ((f32[4,2,128,256]{2,3,1,0:T(8,128)}), f32[4,2,128,256]{2,3,1,0:T(8,128)S(1)}, u32[]{:S(2)}, u32[]{:S(2)}) async-start(f32[4,2,128,256]{2,3,1,0:T(8,128)} %copy.32), calls=%async_computation | async-start | bytes 2097152 | tf_op jit(solution)/shard_map/all_to_all | solution.py:269
  22.6 3.4 %copy-start.1 = (bf16[2048,2048]{1,0:T(8,128)(2,1)S(1)}, bf16[2048,2048]{1,0:T(8,128)(2,1)}, u32[]{:S(2)}) copy-start(bf16[2048,2048]{1,0:T(8,128)(2,1)} %constant.38.clone.high_ref) | copy-start | bytes 25165828
  25.9 3.4 %copy-start.2 = (bf16[2048,2048]{1,0:T(8,128)(2,1)S(1)}, bf16[2048,2048]{1,0:T(8,128)(2,1)}, u32[]{:S(2)}) copy-start(bf16[2048,2048]{1,0:T(8,128)(2,1)} %constant.39.clone.low_ref) | copy-start | bytes 25165828
  38.9 29.5 %all-to-all-start.1 = ((f32[4,2,128,256]{3,2,1,0:T(8,128)}), f32[4,2,128,256]{3,2,1,0:T(8,128)}, u32[]{:S(2)}, u32[]{:S(2)}) async-start(f32[4,2,128,256]{3,2,1,0:T(8,128)} %bitcast.3), calls=%async_computation.1 | async-start | bytes 2097152 | tf_op jit(solution)/shard_map/all_to_all | solution.py:281
  44.7 1.2 copy-start.6
  44.7 1.4 copy-start.9
  71.2 1.6 %copy-start.4 = (bf16[1024,1024]{1,0:T(8,128)(2,1)S(1)}, bf16[1024,1024]{1,0:T(8,128)(2,1)}, u32[]{:S(2)}) copy-start(bf16[1024,1024]{1,0:T(8,128)(2,1)} %constant.41.clone) | copy-start | bytes 6291460
  73.9 1.6 %copy-start.3 = (bf16[1024,1024]{1,0:T(8,128)(2,1)S(1)}, bf16[1024,1024]{1,0:T(8,128)(2,1)}, u32[]{:S(2)}) copy-start(bf16[1024,1024]{1,0:T(8,128)(2,1)} %constant.42.clone) | copy-start | bytes 6291460
  83.3 1.2 slice-start.2
  112.5 5.0 %slice-start = ((s8[8388608]{0:T(1024)(128)(4,1)}), s8[4194304]{0:T(1024)(128)(4,1)S(1)}, s32[]{:S(2)}) async-start(s8[8388608]{0:T(1024)(128)(4,1)} %bitcast.113), calls=%async_computation.3 | async-start | bytes 8388608
  112.6 5.7 %slice-start.1 = ((s8[8388608]{0:T(1024)(128)(4,1)}), s8[4194304]{0:T(1024)(128)(4,1)S(1)}, s32[]{:S(2)}) async-start(s8[8388608]{0:T(1024)(128)(4,1)} %bitcast.113), calls=%async_computation.4 | async-start | bytes 8388608
  120.9 1.2 copy-start.8

commit v3 on v2

--- a/solution.py
+++ b/solution.py
@@ -146,6 +146,103 @@
         ),
         compiler_params=pltpu.CompilerParams(vmem_limit_bytes=32 * 1024 * 1024),
     )(image, high, low)
+
+
+def channel_kernel(
+    here_ref, rows_ref, amp_ref, high_ref, low_ref, back_high_ref, back_low_ref, flip_ref, out_ref,
+    in_high, in_low, freq, mid_high, mid_low, upper, *, norm,
+):
+    blocks, _, local, cols = amp_ref.shape
+    channels = blocks * local
+    lane = lax.broadcasted_iota(jnp.int32, (local, 128), 1)
+    for d in range(blocks):
+        real = pl.ds(2 * d * local, local)
+        imag = pl.ds((2 * d + 1) * local, local)
+        for part in (real, imag):
+            in_high[part, :cols], in_low[part, :cols] = split(rows_ref[part, :])
+        edges = jnp.where(lane == 0, rows_ref[real, :1], jnp.where(lane == 1, rows_ref[imag, :1], 0.0))
+        in_high[real, cols:], in_low[real, cols:] = split(edges)
+        in_high[imag, cols:] = jnp.zeros((local, 128), BF16)
+        in_low[imag, cols:] = jnp.zeros((local, 128), BF16)
+        upper[pl.ds(d * local, local), :] = amp_ref[d, 1].astype(BF16)
+
+    def product_of(high, low, part, right_high, right_low):
+        return (
+            dot(high[part, :], right_high[...])
+            + dot(high[part, :], right_low[...])
+            + dot(low[part, :], right_high[...])
+        )
+
+    for tile in range(2 * blocks):
+        part = pl.ds(tile * local, local)
+        freq[part, :] = product_of(high_ref, low_ref, part, in_high, in_low) * norm
+    for d in range(blocks):
+        real = pl.ds(d * local, local)
+        imag = pl.ds(channels + d * local, local)
+        amp_sum = amp_ref[d, 0] + dot(flip_ref[real, :], upper[...])
+        amp_edges = jnp.where(lane == 0, amp_ref[d, 0][:, :1], amp_ref[d, 1][:, :1])
+        for lanes, amp in ((pl.ds(0, cols), amp_sum), (pl.ds(cols, 128), amp_edges)):
+            freq_real = freq[real, lanes]
+            freq_imag = freq[imag, lanes]
+            gain = lax.rsqrt(freq_real * freq_real + freq_imag * freq_imag + 1.0) * amp * norm
+            mid_high[real, lanes], mid_low[real, lanes] = split(freq_real * gain)
+            mid_high[imag, lanes], mid_low[imag, lanes] = split(freq_imag * gain)
+    column = lax.broadcasted_iota(jnp.int32, (local, cols), 1)
+    first = (column + here_ref[0]) == 0
+    for d in range(blocks):
+        real = pl.ds(2 * d * local, local)
+        imag = pl.ds((2 * d + 1) * local, local)
+        back_real = product_of(back_high_ref, back_low_ref, real, mid_high, mid_low)
+        back_imag = product_of(back_high_ref, back_low_ref, imag, mid_high, mid_low)
+        out_ref[real, :] = jnp.where(first, back_real[:, cols : cols + 1], back_real[:, :cols])
+        out_ref[imag, :] = jnp.where(first, back_real[:, cols + 1 : cols + 2], back_imag[:, :cols])
+
+
+def channel_pass(here, rows, amp, norm):
+    blocks, _, local, cols = amp.shape
+    channels = blocks * local
+    table = chan_table(channels, blocks)
+    vmem = pl.BlockSpec(memory_space=pltpu.VMEM)
+    wide = (2 * channels, cols + 128)
+    return pl.pallas_call(
+        partial(channel_kernel, norm=norm),
+        in_specs=[pl.BlockSpec(memory_space=pltpu.SMEM)] + [vmem] * 7,
+        out_specs=vmem,
+        out_shape=jax.ShapeDtypeStruct((2 * channels, cols), F32),
+        scratch_shapes=[
+            pltpu.VMEM(wide, BF16),
+            pltpu.VMEM(wide, BF16),
+            pltpu.VMEM(wide, F32),
+            pltpu.VMEM(wide, BF16),
+            pltpu.VMEM(wide, BF16),
+            pltpu.VMEM((channels, cols), BF16),
+        ],
+        compiler_params=pltpu.CompilerParams(vmem_limit_bytes=40 * 1024 * 1024),
+    )(here.reshape(1), rows, amp, *two_parts(table), *two_parts(np.ascontiguousarray(table.T)), negation(channels))
+
+
+def general_pass(here, spectrum, amp, norm):
+    blocks, _, rows, cols = amp.shape
+    channels = blocks * rows
+    lane = lax.broadcasted_iota(jnp.int32, (1, 128), 1)
+    first_col = spectrum[:, :, :, :1]
+    extra = jnp.where(lane == 0, first_col[:, 0], 0.0) + jnp.where(lane == 1, first_col[:, 1], 0.0)
+    extra = jnp.stack([extra, jnp.zeros_like(extra)], axis=1)
+    stacked = jnp.concatenate([spectrum, extra], axis=3).reshape(2 * channels, cols + 128)
+    amp_low = amp[:, 0].reshape(channels, cols)
+    amp_up = amp[:, 1].reshape(channels, cols)
+    amp_sum = amp_low + dot(negation(channels).astype(F32), amp_up)
+    amp_extra = jnp.where(lane == 0, amp_low[:, :1], amp_up[:, :1])
+    amp_all = jnp.concatenate([amp_sum, amp_extra], axis=1)
+
+    freq = chan_forward(stacked, channels, blocks).reshape(2, channels, cols + 128) * norm
+    inverse_amp = lax.rsqrt(freq[0] * freq[0] + freq[1] * freq[1] + 1.0)
+    scaled = freq * (inverse_amp * amp_all * norm)
+    back = chan_inverse(scaled.reshape(2 * channels, cols + 128), channels, blocks)
+    back = back.reshape(blocks, 2, rows, cols + 128)
+    edge = jnp.stack([back[:, 0, :, cols : cols + 1], back[:, 0, :, cols + 1 : cols + 2]], axis=1)
+    column = lax.broadcasted_iota(jnp.int32, (1, 1, 1, cols), 3)
+    return jnp.where((column == 0) & (here == 0), edge, back[:, :, :, :cols])
 
 
 def reduce_kernel(
@@ -280,25 +377,11 @@
     spectrum, amp = lax.optimization_barrier((spectrum, amp))
     spectrum = lax.all_to_all(spectrum, "chan", split_axis=0, concat_axis=0, tiled=True)
 
-    lane = lax.broadcasted_iota(jnp.int32, (1, 128), 1)
-    first_col = spectrum[:, :, :, :1]
-    extra = jnp.where(lane == 0, first_col[:, 0], 0.0) + jnp.where(lane == 1, first_col[:, 1], 0.0)
-    extra = jnp.stack([extra, jnp.zeros_like(extra)], axis=1)
-    stacked = jnp.concatenate([spectrum, extra], axis=3).reshape(2 * channels, cols + 128)
-    amp_low = amp[:, 0].reshape(channels, cols)
-    amp_up = amp[:, 1].reshape(channels, cols)
-    amp_sum = amp_low + dot(negation(channels).astype(F32), amp_up)
-    amp_extra = jnp.where(lane == 0, amp_low[:, :1], amp_up[:, :1])
-    amp_all = jnp.concatenate([amp_sum, amp_extra], axis=1)
-
-    freq = chan_forward(stacked, channels, blocks).reshape(2, channels, cols + 128) * norm
-    inverse_amp = lax.rsqrt(freq[0] * freq[0] + freq[1] * freq[1] + 1.0)
-    scaled = freq * (inverse_amp * amp_all * norm)
-    back = chan_inverse(scaled.reshape(2 * channels, cols + 128), channels, blocks)
-    back = back.reshape(blocks, 2, rows, cols + 128)
-    edge = jnp.stack([back[:, 0, :, cols : cols + 1], back[:, 0, :, cols + 1 : cols + 2]], axis=1)
-    column = lax.broadcasted_iota(jnp.int32, (1, 1, 1, cols), 3)
-    returned = jnp.where((column == 0) & (here == 0), edge, back[:, :, :, :cols])
+    if channels <= DENSE_LIMIT and cols % 128 == 0:
+        returned = channel_pass(here, spectrum.reshape(2 * channels, cols), amp, norm)
+        returned = returned.reshape(blocks, 2, rows, cols)
+    else:
+        returned = general_pass(here, spectrum, amp, norm)
     returned = lax.all_to_all(returned, "chan", split_axis=0, concat_axis=0, tiled=True)
 
     returned = returned.transpose(2, 0, 1, 3).reshape(rows, samples)

time: 146 us -> 145 us (level)
  Pallas kernels: 28.2 us -> 35.4 us
  matrix products: 16.6 us -> 11.5 us
  local copies, waits for them, and re-layouts: 33 us -> 28.8 us
  waiting for transfers between devices: 24 us -> 27.2 us
    pallas_call x0 -> x1, Pallas kernels: none -> 7.85 us  [channel_pass(): pl.pallas_call(partial(channel_kernel, norm=norm), in_specs=[pl.BlockSpec...]
    dot_general x13 -> x6, matrix products: 16.6 us -> 11.5 us  [dot(): lax.dot_general(left, right, (dims, ((), ())), preferred_element_type=F32)]
    unnamed x30 -> x32, local copies, waits for them, and re-layouts: 13.7 us -> 18.1 us
    all_to_all x1, waiting for transfers between devices: 21.9 us -> 25.1 us  [per_device(): lax.all_to_all(spectrum, 'chan', split_axis=0, concat_axis=0, tiled=True)]
    slice x9 -> x0, local copies, waits for them, and re-layouts: 3.02 us -> none  [the longest x1 1.25 us: per_device(): first_col[:, 0]]
  transfers between devices with their start and end apart: 2 -> 2, of which waited for: 2 -> 2; matrix products, arithmetic and copies ran while one was open for 8% -> 6% of each run, Pallas kernels for 5% -> 5%
where the time goes in v3:
time: 145 us
  Pallas kernels  35.4 us (24%)
  local copies, waits for them, and re-layouts  28.8 us (20%)
  blocking collectives  27.7 us (19%)
  waiting for transfers between devices  27.2 us (19%)
  matrix products  11.5 us (8%)
  starting transfers between devices  10.9 us (8%)
  other arithmetic  2.42 us (2%)
    all_to_all x1, blocking collectives, per_device(): lax.all_to_all(returned, 'chan', split_axis=0, concat_axis=0, tiled=True)  27.7 us
    all_to_all x1, waiting for transfers between devices, per_device(): lax.all_to_all(spectrum, 'chan', split_axis=0, concat_axis=0, tiled=True)  25.1 us
    pallas_call x1, Pallas kernels, reduce_scatter(): pl.pallas_call(reduce_kernel, in_specs=[pl.BlockSpec(memory_space=pltpu.V...  20.8 us
    unnamed x32, local copies, waits for them, and re-layouts  18.1 us
    dot_general x6, matrix products, dot(): lax.dot_general(left, right, (dims, ((), ())), preferred_element_type=F32)  11.5 us
    pallas_call x1, Pallas kernels, channel_pass(): pl.pallas_call(partial(channel_kernel, norm=norm), in_specs=[pl.BlockSpec...  7.85 us
    pallas_call x1, Pallas kernels, time_forward(): pl.pallas_call(time_forward_kernel, grid=(steps,), in_specs=[pl.BlockSpec...  6.71 us
    all_to_all x1, starting transfers between devices, per_device(): amp = lax.all_to_all(amp, 'chan', split_axis=0, concat_axis=0, tiled=True)  6.45 us
  transfers between devices with their start and end apart: 2, of which 2 were waited for; matrix products, arithmetic and copies ran while one was open for 6% of the time, Pallas kernels for 5%

profile of v3, /device:TPU:0, one launch (start us, length us, event | category | flops | bytes accessed | tf_op | source)
XLA Modules:
  0.0 144.7 jit_solution(18178661341923724674)
XLA Ops:
  0.6 1.4 copy.17
  2.1 2.3 %fusion.9 = f32[1024,128]{1,0:T(8,128)S(1)} fusion(bf16[1024,1024]{1,0:T(8,128)(2,1)} %constant.27.clone, bf16[128,2048]{0,1:T(8,128)(2,1)S(1)} %bitcast.62), kind=kOutput, calls=%fused_computation.18 | convolution fusion | flops 268435456 | bytes 2883584 | tf_op jit(solution)/shard_map/dot_general | solution.py:54
  4.8 1.1 maximum_bitcast_fusion
  5.9 6.4 %all-to-all-start = ((f32[4,2,128,256]{3,2,1,0:T(8,128)}), f32[4,2,128,256]{3,2,1,0:T(8,128)S(1)}, u32[]{:S(2)}, u32[]{:S(2)}) async-start(f32[4,2,128,256]{3,2,1,0:T(8,128)} %maximum_bitcast_fusion), calls=%async_computation | async-start | bytes 2097152 | tf_op jit(solution)/shard_map/all_to_all | solution.py:366
  12.6 1.3 reshape.51
  13.9 1.3 convolution_convert_fusion
  15.2 1.8 %reshape.52 = bf16[8,32,16,64]{3,2,1,0:T(8,128)(2,1)S(1)} reshape(bf16[256,1024]{1,0:T(8,128)(2,1)} %convolution_convert_fusion) | data formatting | bytes 1048576 | tf_op jit(solution)/shard_map/reshape | solution.py:369
  16.9 1.3 copy.25
  18.2 2.0 %reshape.53 = bf16[128,2048]{1,0:T(8,128)(2,1)S(1)} reshape(bf16[8,16,32,64]{3,2,1,0:T(8,128)(2,1)} %bitcast.58) | data formatting | bytes 1048576 | tf_op jit(solution)/shard_map/reshape | solution.py:370
  20.3 1.2 bitcast_select_fusion.image_ref
  21.4 3.4 %copy-done.1 = bf16[2048,2048]{1,0:T(8,128)(2,1)S(1)} copy-done((bf16[2048,2048]{1,0:T(8,128)(2,1)S(1)}, bf16[2048,2048]{1,0:T(8,128)(2,1)}, u32[]{:S(2)}) %copy-start.1) | copy-done | bytes 8388632
  24.8 3.4 %copy-done.2 = bf16[2048,2048]{1,0:T(8,128)(2,1)S(1)} copy-done((bf16[2048,2048]{1,0:T(8,128)(2,1)S(1)}, bf16[2048,2048]{1,0:T(8,128)(2,1)}, u32[]{:S(2)}) %copy-start.2) | copy-done | bytes 8388632
  28.2 6.7 %shard_map.140 = f32[8,128,256]{2,1,0:T(8,128)S(1)} custom-call(bf16[128,2048]{1,0:T(8,128)(2,1)S(1)} %bitcast_select_fusion.image_ref, bf16[2048,2048]{1,0:T(8,128)(2,1)S(1)} %copy-done.1, bf16[2048,2048]{1,0:T(8,128)(2,1)S(1)} %copy-done.2), custom_call_target="tpu_custom_call" | custom-call | flops 2147483648 | bytes 16777216 | tf_op jit(solution)/shard_map/pallas_call | solution.py:134
  34.9 1.0 copy-done.3
  35.9 2.1 %all-to-all-done.amp_ref = f32[4,2,128,256]{3,2,1,0:T(8,128)S(1)} async-done(((f32[4,2,128,256]{3,2,1,0:T(8,128)}), f32[4,2,128,256]{3,2,1,0:T(8,128)S(1)}, u32[]{:S(2)}, u32[]{:S(2)}) %all-to-all-start) | async-done | bytes 1048608 | tf_op jit(solution)/shard_map/all_to_all | solution.py:366
  38.0 4.4 %all-to-all-start.1 = ((f32[4,2,128,256]{3,2,1,0:T(8,128)}), f32[4,2,128,256]{3,2,1,0:T(8,128)}, u32[]{:S(2)}, u32[]{:S(2)}) async-start(f32[4,2,128,256]{3,2,1,0:T(8,128)} %bitcast.56), calls=%async_computation.1 | async-start | bytes 2097152 | tf_op jit(solution)/shard_map/all_to_all | solution.py:378
  42.5 25.1 %all-to-all-done.1 = f32[4,2,128,256]{3,2,1,0:T(8,128)} async-done(((f32[4,2,128,256]{3,2,1,0:T(8,128)}), f32[4,2,128,256]{3,2,1,0:T(8,128)}, u32[]{:S(2)}, u32[]{:S(2)}) %all-to-all-start.1) | async-done | bytes 1048608 | tf_op jit(solution)/shard_map/all_to_all | solution.py:378
  67.6 1.6 %copy-done.5 = bf16[1024,1024]{1,0:T(8,128)(2,1)S(1)} copy-done((bf16[1024,1024]{1,0:T(8,128)(2,1)S(1)}, bf16[1024,1024]{1,0:T(8,128)(2,1)}, u32[]{:S(2)}) %copy-start.5) | copy-done | bytes 2097176
  69.2 1.6 %copy-done.6 = bf16[1024,1024]{1,0:T(8,128)(2,1)S(1)} copy-done((bf16[1024,1024]{1,0:T(8,128)(2,1)S(1)}, bf16[1024,1024]{1,0:T(8,128)(2,1)}, u32[]{:S(2)}) %copy-start.6) | copy-done | bytes 2097176
  70.8 1.6 %copy-done.7 = bf16[1024,1024]{1,0:T(8,128)(2,1)S(1)} copy-done((bf16[1024,1024]{1,0:T(8,128)(2,1)S(1)}, bf16[1024,1024]{1,0:T(8,128)(2,1)}, u32[]{:S(2)}) %copy-start.7) | copy-done | bytes 2097176
  72.4 1.6 %copy-done.8 = bf16[1024,1024]{1,0:T(8,128)(2,1)S(1)} copy-done((bf16[1024,1024]{1,0:T(8,128)(2,1)S(1)}, bf16[1024,1024]{1,0:T(8,128)(2,1)}, u32[]{:S(2)}) %copy-start.8) | copy-done | bytes 2097176
  73.9 7.9 %shard_map.141 = f32[1024,256]{1,0:T(8,128)S(1)} custom-call(s32[1]{0:T(128)} %bitcast.3.here_ref, f32[1024,256]{1,0:T(8,128)} %bitcast.10.rows_ref, f32[4,2,128,256]{3,2,1,0:T(8,128)S(1)} %all-to-all-done.amp_ref, bf16[1024,1024]{1,0:T(8,128)(2,1)S(1)} %copy-done.5, bf16[1024,1024]{1,0:T(8,128)(2,1)S(1)} %copy-done.6, bf16[1024,1024]{1,0:T(8,128)(2,1)S(1)} %copy-done.7, ...), custom_call_target="tpu_custom_call" | custom-call | tf_op jit(solution)/shard_map/pallas_call | solution.py:207
  81.8 1.0 copy-done.4
  82.8 1.5 %copy.20 = f32[4,2,128,256]{2,3,1,0:T(8,128)S(1)} copy(f32[4,2,128,256]{3,2,1,0:T(8,128)} %bitcast.57) | data formatting | bytes 2097152 | tf_op jit(solution)/shard_map/reshape | solution.py:382
  84.3 27.7 %all_to_all.15 = f32[4,2,128,256]{2,3,1,0:T(8,128)S(1)} all-to-all(f32[4,2,128,256]{2,3,1,0:T(8,128)S(1)} %copy.20), channel_id=1, replica_groups=mesh['groups'=2,'chan'=4,'win'=4] {'chan'}, dimensions={0} | all-to-all | bytes 2097152 | tf_op jit(solution)/shard_map/all_to_all | solution.py:385
  112.2 4.8 %fusion.11 = f32[128,2048]{1,0:T(8,128)S(1)} fusion(bf16[128,2048]{0,1:T(8,128)(2,1)S(1)} %get-tuple-element.7, bf16[2048,2048]{1,0:T(8,128)(2,1)} %constant.28.clone.high_ref), kind=kOutput, calls=%fused_computation.21 | convolution fusion | flops 1073741824 | bytes 9961472 | tf_op jit(solution)/shard_map/dot_general | solution.py:54
  117.0 0.9 slice-done.1
  117.9 1.4 fusion.3
  119.3 1.1 reshape.59
  120.8 0.7 reshape.60
  122.1 1.2 fusion.4
  123.3 20.8 %shard_map.142 = f32[128,256]{1,0:T(8,128)S(1)} custom-call(f32[4,128,1024]{2,1,0:T(8,128)S(1)} %bitcast.55), custom_call_target="tpu_custom_call" | custom-call | tf_op jit(solution)/shard_map/pallas_call | solution.py:324
  (32 shorter events, 2.4 us)
Async XLA Ops:
  0.6 13.3 %copy-start = (bf16[512,1024]{1,0:T(8,128)(2,1)S(1)}, bf16[512,1024]{1,0:T(8,128)(2,1)}, u32[]{:S(2)}) copy-start(bf16[512,1024]{1,0:T(8,128)(2,1)} %param.14) | copy-start | bytes 3145732
  4.8 7.6 %copy-start.12 = (s32[1,256]{1,0:T(1,128)S(1)}, s32[1,256]{1,0:T(1,128)}, u32[]{:S(2)}) copy-start(s32[1,256]{1,0:T(1,128)} %param.17) | copy-start | bytes 3076
  5.9 8.1 %copy-start.10 = (bf16[1,256,512]{2,1,0:T(8,128)(2,1)S(1)}, bf16[1,256,512]{2,1,0:T(8,128)(2,1)}, u32[]{:S(2)}) copy-start(bf16[1,256,512]{2,1,0:T(8,128)(2,1)} %param.13) | copy-start | bytes 786436
  5.9 32.2 %all-to-all-start = ((f32[4,2,128,256]{3,2,1,0:T(8,128)}), f32[4,2,128,256]{3,2,1,0:T(8,128)S(1)}, u32[]{:S(2)}, u32[]{:S(2)}) async-start(f32[4,2,128,256]{3,2,1,0:T(8,128)} %maximum_bitcast_fusion), calls=%async_computation | async-start | bytes 2097152 | tf_op jit(solution)/shard_map/all_to_all | solution.py:366
  21.4 3.4 %copy-start.1 = (bf16[2048,2048]{1,0:T(8,128)(2,1)S(1)}, bf16[2048,2048]{1,0:T(8,128)(2,1)}, u32[]{:S(2)}) copy-start(bf16[2048,2048]{1,0:T(8,128)(2,1)} %constant.28.clone.high_ref) | copy-start | bytes 25165828
  24.8 3.4 %copy-start.2 = (bf16[2048,2048]{1,0:T(8,128)(2,1)S(1)}, bf16[2048,2048]{1,0:T(8,128)(2,1)}, u32[]{:S(2)}) copy-start(bf16[2048,2048]{1,0:T(8,128)(2,1)} %constant.29.clone.low_ref) | copy-start | bytes 25165828
  34.9 1.0 copy-start.3
  35.9 31.7 %copy-start.9 = (bf16[512,512]{1,0:T(8,128)(2,1)S(1)}, bf16[512,512]{1,0:T(8,128)(2,1)}, u32[]{:S(2)}) copy-start(bf16[512,512]{1,0:T(8,128)(2,1)} %constant.34.clone.flip_ref) | copy-start | bytes 1572868
  38.0 29.5 %all-to-all-start.1 = ((f32[4,2,128,256]{3,2,1,0:T(8,128)}), f32[4,2,128,256]{3,2,1,0:T(8,128)}, u32[]{:S(2)}, u32[]{:S(2)}) async-start(f32[4,2,128,256]{3,2,1,0:T(8,128)} %bitcast.56), calls=%async_computation.1 | async-start | bytes 2097152 | tf_op jit(solution)/shard_map/all_to_all | solution.py:378
  67.6 1.6 %copy-start.5 = (bf16[1024,1024]{1,0:T(8,128)(2,1)S(1)}, bf16[1024,1024]{1,0:T(8,128)(2,1)}, u32[]{:S(2)}) copy-start(bf16[1024,1024]{1,0:T(8,128)(2,1)} %constant.30.clone.high_ref) | copy-start | bytes 6291460
  69.2 1.6 %copy-start.6 = (bf16[1024,1024]{1,0:T(8,128)(2,1)S(1)}, bf16[1024,1024]{1,0:T(8,128)(2,1)}, u32[]{:S(2)}) copy-start(bf16[1024,1024]{1,0:T(8,128)(2,1)} %constant.31.clone.low_ref) | copy-start | bytes 6291460
  70.8 1.6 %copy-start.7 = (bf16[1024,1024]{1,0:T(8,128)(2,1)S(1)}, bf16[1024,1024]{1,0:T(8,128)(2,1)}, u32[]{:S(2)}) copy-start(bf16[1024,1024]{1,0:T(8,128)(2,1)} %constant.32.clone.back_high_ref) | copy-start | bytes 6291460
  72.4 1.6 %copy-start.8 = (bf16[1024,1024]{1,0:T(8,128)(2,1)S(1)}, bf16[1024,1024]{1,0:T(8,128)(2,1)}, u32[]{:S(2)}) copy-start(bf16[1024,1024]{1,0:T(8,128)(2,1)} %constant.33.clone.back_low_ref) | copy-start | bytes 6291460
  81.8 1.0 copy-start.4
  112.0 5.0 %slice-start = ((s8[8388608]{0:T(1024)(128)(4,1)}), s8[4194304]{0:T(1024)(128)(4,1)S(1)}, s32[]{:S(2)}) async-start(s8[8388608]{0:T(1024)(128)(4,1)} %bitcast.53), calls=%async_computation.3 | async-start | bytes 8388608
  112.2 5.7 %slice-start.1 = ((s8[8388608]{0:T(1024)(128)(4,1)}), s8[4194304]{0:T(1024)(128)(4,1)S(1)}, s32[]{:S(2)}) async-start(s8[8388608]{0:T(1024)(128)(4,1)} %bitcast.53), calls=%async_computation.4 | async-start | bytes 8388608
  120.4 1.2 copy-start.11

commit v4 on v3

--- a/solution.py
+++ b/solution.py
@@ -149,7 +149,7 @@
 
 
 def channel_kernel(
-    here_ref, rows_ref, amp_ref, high_ref, low_ref, back_high_ref, back_low_ref, flip_ref, out_ref,
+    here_ref, rows_ref, amp_ref, high_ref, low_ref, flip_ref, out_ref,
     in_high, in_low, freq, mid_high, mid_low, upper, *, norm,
 ):
     blocks, _, local, cols = amp_ref.shape
@@ -166,16 +166,11 @@
         in_low[imag, cols:] = jnp.zeros((local, 128), BF16)
         upper[pl.ds(d * local, local), :] = amp_ref[d, 1].astype(BF16)
 
-    def product_of(high, low, part, right_high, right_low):
-        return (
-            dot(high[part, :], right_high[...])
-            + dot(high[part, :], right_low[...])
-            + dot(low[part, :], right_high[...])
-        )
-
     for tile in range(2 * blocks):
         part = pl.ds(tile * local, local)
-        freq[part, :] = product_of(high_ref, low_ref, part, in_high, in_low) * norm
+        table = high_ref[part, :]
+        total = dot(table, in_high[...]) + dot(table, in_low[...]) + dot(low_ref[part, :], in_high[...])
+        freq[part, :] = total * norm
     for d in range(blocks):
         real = pl.ds(d * local, local)
         imag = pl.ds(channels + d * local, local)
@@ -192,8 +187,9 @@
     for d in range(blocks):
         real = pl.ds(2 * d * local, local)
         imag = pl.ds((2 * d + 1) * local, local)
-        back_real = product_of(back_high_ref, back_low_ref, real, mid_high, mid_low)
-        back_imag = product_of(back_high_ref, back_low_ref, imag, mid_high, mid_low)
+        down = ((0,), (0,))
+        back_real = dot(high_ref[:, real], mid_high[...], down) + dot(high_ref[:, real], mid_low[...], down)
+        back_imag = dot(high_ref[:, imag], mid_high[...], down) + dot(high_ref[:, imag], mid_low[...], down)
         out_ref[real, :] = jnp.where(first, back_real[:, cols : cols + 1], back_real[:, :cols])
         out_ref[imag, :] = jnp.where(first, back_real[:, cols + 1 : cols + 2], back_imag[:, :cols])
 
@@ -206,7 +202,7 @@
     wide = (2 * channels, cols + 128)
     return pl.pallas_call(
         partial(channel_kernel, norm=norm),
-        in_specs=[pl.BlockSpec(memory_space=pltpu.SMEM)] + [vmem] * 7,
+        in_specs=[pl.BlockSpec(memory_space=pltpu.SMEM)] + [vmem] * 5,
         out_specs=vmem,
         out_shape=jax.ShapeDtypeStruct((2 * channels, cols), F32),
         scratch_shapes=[
@@ -218,7 +214,29 @@
             pltpu.VMEM((channels, cols), BF16),
         ],
         compiler_params=pltpu.CompilerParams(vmem_limit_bytes=40 * 1024 * 1024),
-    )(here.reshape(1), rows, amp, *two_parts(table), *two_parts(np.ascontiguousarray(table.T)), negation(channels))
+    )(here.reshape(1), rows, amp, *two_parts(table), negation(channels))
+
+
+def amp_kernel(lower_ref, upper_ref, flip_ref, out_ref):
+    out_ref[0, 0] = lower_ref[...].astype(F32)
+    out_ref[0, 1] = dot(upper_ref[...], flip_ref[...])
+
+
+def amp_blocks(target_amp, blocks):
+    rows, samples = target_amp.shape
+    half = samples // 2
+    cols = half // blocks
+    return pl.pallas_call(
+        amp_kernel,
+        grid=(blocks,),
+        in_specs=[
+            pl.BlockSpec((rows, cols), lambda i: (0, i)),
+            pl.BlockSpec((rows, half), lambda i: (0, 1)),
+            pl.BlockSpec((half, cols), lambda i: (0, i)),
+        ],
+        out_specs=pl.BlockSpec((1, 2, rows, cols), lambda i: (i, 0, 0, 0)),
+        out_shape=jax.ShapeDtypeStruct((blocks, 2, rows, cols), F32),
+    )(target_amp, target_amp, negation(half))
 
 
 def general_pass(here, spectrum, amp, norm):
@@ -360,9 +378,12 @@
     norm = 1.0 / math.sqrt(channels * samples)
     here = lax.axis_index("chan")
 
-    upper = dot(target_amp[:, half:], negation(half))
-    amp = jnp.stack([target_amp[:, :half].astype(F32), upper])
-    amp = amp.reshape(2, rows, blocks, cols).transpose(2, 0, 1, 3)
+    if cols % 128 == 0:
+        amp = amp_blocks(target_amp, blocks)
+    else:
+        upper = dot(target_amp[:, half:], negation(half))
+        amp = jnp.stack([target_amp[:, :half].astype(F32), upper])
+        amp = amp.reshape(2, rows, blocks, cols).transpose(2, 0, 1, 3)
     amp = lax.all_to_all(amp, "chan", split_axis=0, concat_axis=0, tiled=True)
 
     patches = dot(tokens, head_weight).astype(BF16)

time: 145 us -> 142 us (0.979)
  local copies, waits for them, and re-layouts: 28.8 us -> 23.8 us
  Pallas kernels: 35.4 us -> 38.9 us
    unnamed x32 -> x21, local copies, waits for them, and re-layouts: 18.1 us -> 13.5 us
    pallas_call x0 -> x1, Pallas kernels: none -> 4.26 us  [amp_blocks(): pl.pallas_call(amp_kernel, grid=(blocks,), in_specs=[pl.BlockSpec((rows,...]
    all_to_all x1, waiting for transfers between devices: 2.14 us -> 0.49 us  [per_device(): amp = lax.all_to_all(amp, 'chan', split_axis=0, concat_axis=0, tiled=True)]
    dot_general x6 -> x5, matrix products: 11.5 us -> 11.1 us  [dot(): lax.dot_general(left, right, (dims, ((), ())), preferred_element_type=F32)]
  transfers between devices with their start and end apart: 2 -> 2, of which waited for: 2 -> 2; matrix products, arithmetic and copies ran while one was open for 6% -> 8% of each run, Pallas kernels for 5% -> 5%
where the time goes in v4:
time: 142 us; the launch traced here: 141 us
  Pallas kernels  38.9 us (27%)
  blocking collectives  27.7 us (20%)
  waiting for transfers between devices  25.8 us (18%)
  local copies, waits for them, and re-layouts  23.8 us (17%)
  matrix products  11.1 us (8%)
  starting transfers between devices  10.9 us (8%)
  other arithmetic  2 us (1%)
    all_to_all x1, blocking collectives, per_device(): lax.all_to_all(returned, 'chan', split_axis=0, concat_axis=0, tiled=True)  27.7 us
    all_to_all x1, waiting for transfers between devices, per_device(): lax.all_to_all(spectrum, 'chan', split_axis=0, concat_axis=0, tiled=True)  25.3 us
    pallas_call x1, Pallas kernels, reduce_scatter(): pl.pallas_call(reduce_kernel, in_specs=[pl.BlockSpec(memory_space=pltpu.V...  20.8 us
    unnamed x21, local copies, waits for them, and re-layouts  13.5 us
    dot_general x5, matrix products, dot(): lax.dot_general(left, right, (dims, ((), ())), preferred_element_type=F32)  11.1 us
    pallas_call x1, Pallas kernels, channel_pass(): pl.pallas_call(partial(channel_kernel, norm=norm), in_specs=[pl.BlockSpec...  7.14 us
    pallas_call x1, Pallas kernels, time_forward(): pl.pallas_call(time_forward_kernel, grid=(steps,), in_specs=[pl.BlockSpec...  6.71 us
    all_to_all x1, starting transfers between devices, per_device(): amp = lax.all_to_all(amp, 'chan', split_axis=0, concat_axis=0, tiled=True)  6.32 us
  transfers between devices with their start and end apart: 2, of which 2 were waited for; matrix products, arithmetic and copies ran while one was open for 8% of the time, Pallas kernels for 5%

profile of v4, /device:TPU:0, one launch (start us, length us, event | category | flops | bytes accessed | tf_op | source)
XLA Modules:
  0.0 141.0 jit_solution(16201856210319105107)
XLA Ops:
  0.6 4.3 %shard_map.123 = f32[4,2,128,256]{3,2,1,0:T(8,128)} custom-call(bf16[128,2048]{1,0:T(8,128)(2,1)} %bitcast.52, bf16[128,2048]{1,0:T(8,128)(2,1)} %bitcast.53, bf16[1024,1024]{1,0:T(8,128)(2,1)} %constant.23.clone.flip_ref), custom_call_target="tpu_custom_call" | custom-call | tf_op jit(solution)/shard_map/pallas_call | solution.py:229
  4.9 6.3 %all-to-all-start = ((f32[4,2,128,256]{3,2,1,0:T(8,128)}), f32[4,2,128,256]{3,2,1,0:T(8,128)S(1)}, u32[]{:S(2)}, u32[]{:S(2)}) async-start(f32[4,2,128,256]{3,2,1,0:T(8,128)} %shard_map.123), calls=%async_computation | async-start | bytes 2097152 | tf_op jit(solution)/shard_map/all_to_all | solution.py:387
  11.2 0.7 compare_reduce_fusion
  12.2 1.3 reshape.45
  13.5 2.2 %convolution_convert_fusion = bf16[256,1024]{1,0:T(8,128)(2,1)} fusion(bf16[512,1024]{1,0:T(8,128)(2,1)S(1)} %copy-done, bf16[1,256,512]{2,1,0:T(8,128)(2,1)} %param.11), kind=kOutput, calls=%fused_computation.5 | convolution fusion | flops 268697600 | bytes 1835008 | tf_op jit(solution)/shard_map/dot_general | solution.py:54
  15.7 1.8 %reshape.46 = bf16[8,32,16,64]{3,2,1,0:T(8,128)(2,1)S(1)} reshape(bf16[256,1024]{1,0:T(8,128)(2,1)} %convolution_convert_fusion) | data formatting | bytes 1048576 | tf_op jit(solution)/shard_map/reshape | solution.py:390
  17.5 1.3 copy.20
  18.8 2.0 %reshape.47 = bf16[128,2048]{1,0:T(8,128)(2,1)S(1)} reshape(bf16[8,16,32,64]{3,2,1,0:T(8,128)(2,1)} %bitcast.50) | data formatting | bytes 1048576 | tf_op jit(solution)/shard_map/reshape | solution.py:391
  20.8 1.2 bitcast_select_fusion.image_ref
  22.0 3.4 %copy-done.1 = bf16[2048,2048]{1,0:T(8,128)(2,1)S(1)} copy-done((bf16[2048,2048]{1,0:T(8,128)(2,1)S(1)}, bf16[2048,2048]{1,0:T(8,128)(2,1)}, u32[]{:S(2)}) %copy-start.1) | copy-done | bytes 8388632
  25.4 3.4 %copy-done.2 = bf16[2048,2048]{1,0:T(8,128)(2,1)S(1)} copy-done((bf16[2048,2048]{1,0:T(8,128)(2,1)S(1)}, bf16[2048,2048]{1,0:T(8,128)(2,1)}, u32[]{:S(2)}) %copy-start.2) | copy-done | bytes 8388632
  28.7 6.7 %shard_map.122 = f32[8,128,256]{2,1,0:T(8,128)S(1)} custom-call(bf16[128,2048]{1,0:T(8,128)(2,1)S(1)} %bitcast_select_fusion.image_ref, bf16[2048,2048]{1,0:T(8,128)(2,1)S(1)} %copy-done.1, bf16[2048,2048]{1,0:T(8,128)(2,1)S(1)} %copy-done.2), custom_call_target="tpu_custom_call" | custom-call | flops 2147483648 | bytes 16777216 | tf_op jit(solution)/shard_map/pallas_call | solution.py:134
  35.5 1.0 copy-done.3
  36.5 0.5 all-to-all-done.amp_ref
  37.0 4.6 %all-to-all-start.1 = ((f32[4,2,128,256]{3,2,1,0:T(8,128)}), f32[4,2,128,256]{3,2,1,0:T(8,128)}, u32[]{:S(2)}, u32[]{:S(2)}) async-start(f32[4,2,128,256]{3,2,1,0:T(8,128)} %bitcast.48), calls=%async_computation.1 | async-start | bytes 2097152 | tf_op jit(solution)/shard_map/all_to_all | solution.py:399
  41.6 25.3 %all-to-all-done.1 = f32[4,2,128,256]{3,2,1,0:T(8,128)} async-done(((f32[4,2,128,256]{3,2,1,0:T(8,128)}), f32[4,2,128,256]{3,2,1,0:T(8,128)}, u32[]{:S(2)}, u32[]{:S(2)}) %all-to-all-start.1) | async-done | bytes 1048608 | tf_op jit(solution)/shard_map/all_to_all | solution.py:399
  66.8 1.6 %copy-done.5 = bf16[1024,1024]{1,0:T(8,128)(2,1)S(1)} copy-done((bf16[1024,1024]{1,0:T(8,128)(2,1)S(1)}, bf16[1024,1024]{1,0:T(8,128)(2,1)}, u32[]{:S(2)}) %copy-start.5) | copy-done | bytes 2097176
  68.4 1.6 %copy-done.6 = bf16[1024,1024]{1,0:T(8,128)(2,1)S(1)} copy-done((bf16[1024,1024]{1,0:T(8,128)(2,1)S(1)}, bf16[1024,1024]{1,0:T(8,128)(2,1)}, u32[]{:S(2)}) %copy-start.6) | copy-done | bytes 2097176
  70.0 7.1 %shard_map.124 = f32[1024,256]{1,0:T(8,128)S(1)} custom-call(s32[1]{0:T(128)} %bitcast.3.here_ref, f32[1024,256]{1,0:T(8,128)} %bitcast.6.rows_ref, f32[4,2,128,256]{3,2,1,0:T(8,128)S(1)} %all-to-all-done.amp_ref, bf16[1024,1024]{1,0:T(8,128)(2,1)S(1)} %copy-done.5, bf16[1024,1024]{1,0:T(8,128)(2,1)S(1)} %copy-done.6, bf16[512,512]{1,0:T(8,128)(2,1)S(1)} %copy-done.7), custom_call_target="tpu_custom_call" | custom-call | tf_op jit(solution)/shard_map/pallas_call | solution.py:203
  77.2 1.0 copy-done.4
  78.1 1.5 %copy.15 = f32[4,2,128,256]{2,3,1,0:T(8,128)S(1)} copy(f32[4,2,128,256]{3,2,1,0:T(8,128)} %bitcast.49) | data formatting | bytes 2097152 | tf_op jit(solution)/shard_map/reshape | solution.py:403
  79.7 27.7 %all_to_all.15 = f32[4,2,128,256]{2,3,1,0:T(8,128)S(1)} all-to-all(f32[4,2,128,256]{2,3,1,0:T(8,128)S(1)} %copy.15), channel_id=1, replica_groups=mesh['groups'=2,'chan'=4,'win'=4] {'chan'}, dimensions={0} | all-to-all | bytes 2097152 | tf_op jit(solution)/shard_map/all_to_all | solution.py:406
  107.5 4.8 %fusion.9 = f32[128,2048]{1,0:T(8,128)S(1)} fusion(bf16[128,2048]{0,1:T(8,128)(2,1)S(1)} %get-tuple-element.7, bf16[2048,2048]{1,0:T(8,128)(2,1)} %constant.24.clone.high_ref), kind=kOutput, calls=%fused_computation.18 | convolution fusion | flops 1073741824 | bytes 9961472 | tf_op jit(solution)/shard_map/dot_general | solution.py:54
  112.4 0.9 slice-done.1
  113.3 1.4 %fusion.3 = bf16[128,2048]{1,0:T(8,128)(2,1)S(1)} fusion(pred[128,2048]{1,0:T(32,128)(4,1)S(1)} %reshape.45, f32[128,2048]{1,0:T(8,128)S(1)} %fusion.9, bf16[128,2048]{0,1:T(8,128)(2,1)S(1)} %get-tuple-element.6, bf16[2048,2048]{1,0:T(8,128)(2,1)S(1)} %bitcast.46, bf16[128,2048]{1,0:T(8,128)(2,1)S(1)} %bitcast_select_fusion.image_ref), kind=kOutput, calls=%fused_computation.4 | convolution fusion | flops 1075314688 | bytes 11272192 | tf_op jit(solution)/shard_map/dot_general | solution.py:54
  114.7 1.1 reshape.53
  115.8 0.4 copy.19
  116.2 0.7 reshape.54
  116.9 1.4 %fusion.6 = f32[1024,512]{0,1:T(8,128)S(1)} fusion(bf16[256,1024]{1,0:T(8,128)(2,1)S(1)} %reshape.54, bf16[1,256,512]{2,1,0:T(8,128)(2,1)} %param.11), kind=kOutput, calls=%fused_computation.14 | convolution fusion | flops 268435456 | bytes 2883584 | tf_op jit(solution)/shard_map/dot_general | solution.py:54
  118.4 1.2 fusion.4
  119.5 20.8 %shard_map.125 = f32[128,256]{1,0:T(8,128)S(1)} custom-call(f32[4,128,1024]{2,1,0:T(8,128)S(1)} %bitcast.47), custom_call_target="tpu_custom_call" | custom-call | tf_op jit(solution)/shard_map/pallas_call | solution.py:342
  140.4 0.7 copy.24
  (17 shorter events, 0.5 us)
Async XLA Ops:
  0.6 12.9 %copy-start = (bf16[512,1024]{1,0:T(8,128)(2,1)S(1)}, bf16[512,1024]{1,0:T(8,128)(2,1)}, u32[]{:S(2)}) copy-start(bf16[512,1024]{1,0:T(8,128)(2,1)} %param.12) | copy-start | bytes 3145732
  4.9 32.0 %all-to-all-start = ((f32[4,2,128,256]{3,2,1,0:T(8,128)}), f32[4,2,128,256]{3,2,1,0:T(8,128)S(1)}, u32[]{:S(2)}, u32[]{:S(2)}) async-start(f32[4,2,128,256]{3,2,1,0:T(8,128)} %shard_map.123), calls=%async_computation | async-start | bytes 2097152 | tf_op jit(solution)/shard_map/all_to_all | solution.py:387
  22.0 3.4 %copy-start.1 = (bf16[2048,2048]{1,0:T(8,128)(2,1)S(1)}, bf16[2048,2048]{1,0:T(8,128)(2,1)}, u32[]{:S(2)}) copy-start(bf16[2048,2048]{1,0:T(8,128)(2,1)} %constant.24.clone.high_ref) | copy-start | bytes 25165828
  25.4 3.4 %copy-start.2 = (bf16[2048,2048]{1,0:T(8,128)(2,1)S(1)}, bf16[2048,2048]{1,0:T(8,128)(2,1)}, u32[]{:S(2)}) copy-start(bf16[2048,2048]{1,0:T(8,128)(2,1)} %constant.25.clone.low_ref) | copy-start | bytes 25165828
  28.7 38.1 %copy-start.7 = (bf16[512,512]{1,0:T(8,128)(2,1)S(1)}, bf16[512,512]{1,0:T(8,128)(2,1)}, u32[]{:S(2)}) copy-start(bf16[512,512]{1,0:T(8,128)(2,1)} %constant.28.clone.flip_ref) | copy-start | bytes 1572868
  35.5 1.0 copy-start.3
  37.0 29.9 %all-to-all-start.1 = ((f32[4,2,128,256]{3,2,1,0:T(8,128)}), f32[4,2,128,256]{3,2,1,0:T(8,128)}, u32[]{:S(2)}, u32[]{:S(2)}) async-start(f32[4,2,128,256]{3,2,1,0:T(8,128)} %bitcast.48), calls=%async_computation.1 | async-start | bytes 2097152 | tf_op jit(solution)/shard_map/all_to_all | solution.py:399
  66.8 1.6 %copy-start.5 = (bf16[1024,1024]{1,0:T(8,128)(2,1)S(1)}, bf16[1024,1024]{1,0:T(8,128)(2,1)}, u32[]{:S(2)}) copy-start(bf16[1024,1024]{1,0:T(8,128)(2,1)} %constant.26.clone.high_ref) | copy-start | bytes 6291460
  68.4 1.6 %copy-start.6 = (bf16[1024,1024]{1,0:T(8,128)(2,1)S(1)}, bf16[1024,1024]{1,0:T(8,128)(2,1)}, u32[]{:S(2)}) copy-start(bf16[1024,1024]{1,0:T(8,128)(2,1)} %constant.27.clone.low_ref) | copy-start | bytes 6291460
  77.2 1.0 copy-start.4
  107.4 5.0 %slice-start = ((s8[8388608]{0:T(1024)(128)(4,1)}), s8[4194304]{0:T(1024)(128)(4,1)S(1)}, s32[]{:S(2)}) async-start(s8[8388608]{0:T(1024)(128)(4,1)} %bitcast.45), calls=%async_computation.3 | async-start | bytes 8388608
  107.5 5.7 %slice-start.1 = ((s8[8388608]{0:T(1024)(128)(4,1)}), s8[4194304]{0:T(1024)(128)(4,1)S(1)}, s32[]{:S(2)}) async-start(s8[8388608]{0:T(1024)(128)(4,1)} %bitcast.45), calls=%async_computation.4 | async-start | bytes 8388608
